TPU v7x, 256 devices: a whole 4x4x8 slice. The times are simulated.
256 devices in a mesh: seq: 32 (over z, x), head: 8 (over y, core).
Axes of the slice: x: 4, y: 4, z: 8, core: 2. Of those that a mesh axis runs over, the one named last changes fastest.
Arguments:
- queries: bfloat16 [32768, 2048], P('seq', 'head'), may hold values from -80 to 80
- keys: bfloat16 [32768, 2048], P('seq', 'head'), may hold values from -8 to 8
- values: bfloat16 [32768, 2048], P('seq', 'head'), may hold values from -6 to 6
- out_grad: bfloat16 [32768, 2048], P('seq', 'head'), may hold values from -6 to 6
- members: int32 [16, 32, 1024], P('head', 'seq'), may hold values from 0 to 32767, as said below
- centroids: float32 [16, 32, 128], P('head', 'seq'), may hold values from -6 to 6
- proj_weight: bfloat16 [3, 2048, 2048], P(None, None, 'head'), may hold values from -0.125 to 0.125
Outputs:
- input_grad: bfloat16 [32768, 2048], P('seq', 'head')
- new_centroids: float32 [16, 32, 128], P('head', 'seq')
Inputs may be any that keep to these rules, and one draw needn't show every extreme that they name: members[h, c] holds 1024 token indices in increasing order; every token lies in exactly one cluster of each head; at most 64 of the tokens of one index of seq (rows k * 1024 to (k + 1) * 1024 - 1) lie in one cluster of one head, and in every head some cluster takes exactly 64 of them.
All inputs are finite; a program needn't handle non-finite values.
Results may differ from a plain program's by a relative error of at most 0.017.
Values may be sent and summed in bfloat16 or wider, within the bound.
A program may use at most 64 MiB of HBM per device.

v0:
```python
import math

import jax
import jax.numpy as jnp
from jax import lax
from jax.sharding import PartitionSpec as P

decay_rate = 0.99


def as_sent(shard):
    return jax.tree.map(lambda a: a.astype(jnp.bfloat16) if a.dtype == jnp.float32 else a, shard)


def cluster_backward(query_rows, key_rows, value_rows, grad_rows):
    cluster_width, head_width = query_rows.shape
    score_scale = 1.0 / math.sqrt(head_width)
    block_rows = min(512, cluster_width)
    key_total = jnp.zeros((cluster_width, head_width), jnp.float32)
    value_total = jnp.zeros((cluster_width, head_width), jnp.float32)
    pieces = []
    for block_pos in range(cluster_width // block_rows):
        row_low = block_pos * block_rows
        row_high = row_low + block_rows
        query_block = query_rows[row_low:row_high]
        grad_block = grad_rows[row_low:row_high]
        key_prefix = key_rows[:row_high]
        value_prefix = value_rows[:row_high]
        scores = (
            lax.dot_general(
                query_block,
                key_prefix,
                (((1,), (1,)), ((), ())),
                preferred_element_type=jnp.float32,
            )
            * score_scale
        )
        causal = jnp.arange(row_high)[None, :] <= (row_low + jnp.arange(block_rows))[:, None]
        scores = jnp.where(causal, scores, -jnp.inf)
        attn_probs = jax.nn.softmax(scores, axis=-1)
        probs_low = attn_probs.astype(jnp.bfloat16)
        output = jnp.dot(probs_low, value_prefix, preferred_element_type=jnp.float32)
        row_delta = jnp.sum(grad_block.astype(jnp.float32) * output, axis=1, keepdims=True)
        prob_grad = lax.dot_general(
            grad_block, value_prefix, (((1,), (1,)), ((), ())), preferred_element_type=jnp.float32
        )
        score_grad = (attn_probs * (prob_grad - row_delta)).astype(jnp.bfloat16)
        pieces.append(
            (
                jnp.dot(score_grad, key_prefix, preferred_element_type=jnp.float32) * score_scale
            ).astype(jnp.bfloat16)
        )
        key_total = key_total.at[:row_high].add(
            lax.dot_general(
                score_grad,
                query_block,
                (((0,), (0,)), ((), ())),
                preferred_element_type=jnp.float32,
            )
        )
        value_total = value_total.at[:row_high].add(
            lax.dot_general(
                probs_low, grad_block, (((0,), (0,)), ((), ())), preferred_element_type=jnp.float32
            )
        )
    return (
        jnp.concatenate(pieces, axis=0),
        (key_total * score_scale).astype(jnp.bfloat16),
        value_total.astype(jnp.bfloat16),
    )


def shards(queries, keys, values, out_grad, members, centroids, proj_weight):
    seq_count = lax.axis_size("seq")
    seq_index = lax.axis_index("seq")
    tok_rows, columns = queries.shape
    heads_here, clus_here, cluster_width = members.shape
    head_width = columns // heads_here
    capacity = 2 * cluster_width // seq_count
    sources = jnp.arange(seq_count, dtype=jnp.int32)
    slot_ids = jnp.arange(capacity, dtype=jnp.int32)
    owner_rows = members // tok_rows
    counts = jnp.sum((owner_rows[..., None] == sources).astype(jnp.int32), axis=2)
    run_ends = jnp.cumsum(counts, axis=-1)
    run_starts = run_ends - counts
    everything = lax.all_gather(members, "seq", axis=1, tiled=True)
    home_rows = everything // tok_rows
    own_count = jnp.sum((home_rows == seq_index).astype(jnp.int32), axis=-1)
    own_start = jnp.sum((home_rows < seq_index).astype(jnp.int32), axis=-1)
    spots = own_start[..., None] + slot_ids
    picked = jnp.take_along_axis(everything, jnp.clip(spots, 0, cluster_width - 1), axis=2)
    local_rows = jnp.where(slot_ids < own_count[..., None], picked - seq_index * tok_rows, tok_rows)
    wanted = jnp.transpose(
        local_rows.reshape(heads_here, seq_count, clus_here, capacity), (1, 0, 2, 3)
    )
    table = jnp.stack([queries, keys, values, out_grad], axis=1).reshape(
        tok_rows, 4, heads_here, head_width
    )
    table = jnp.transpose(table, (2, 0, 1, 3)).reshape(heads_here, tok_rows, 4 * head_width)
    table = jnp.concatenate(
        [table, jnp.zeros((heads_here, 1, 4 * head_width), jnp.bfloat16)], axis=1
    )
    table = table.reshape(heads_here * (tok_rows + 1), 4 * head_width)
    flat_index = (
        wanted + (jnp.arange(heads_here, dtype=jnp.int32) * (tok_rows + 1))[None, :, None, None]
    )
    payload = jnp.take(table, flat_index, axis=0)
    arrived = lax.all_to_all(payload, "seq", split_axis=0, concat_axis=0, tiled=True)
    head_local = arrived.shape[1]
    pooled = jnp.transpose(arrived, (1, 2, 0, 3, 4)).reshape(
        head_local, clus_here, seq_count * capacity, 4 * head_width
    )
    key_sums = jnp.sum(pooled[..., : 2 * head_width], axis=2, dtype=jnp.float32)
    moved_cent = decay_rate * centroids + 0.5 * (1.0 - decay_rate) * (
        key_sums[..., :head_width] + key_sums[..., head_width:]
    )
    place_ids = jnp.arange(cluster_width, dtype=jnp.int32)
    source_of = jnp.sum((run_ends[..., None, :] <= place_ids[:, None]).astype(jnp.int32), axis=-1)
    offset = place_ids - jnp.take_along_axis(run_starts, source_of, axis=2)
    ordered = jnp.take_along_axis(pooled, (source_of * capacity + offset)[..., None], axis=2)
    flat_rows = ordered.reshape(head_local * clus_here, cluster_width, 4 * head_width)

    def run_cluster(rows):
        query_grad, key_grad, value_grad = cluster_backward(
            rows[:, :head_width],
            rows[:, head_width : 2 * head_width],
            rows[:, 2 * head_width : 3 * head_width],
            rows[:, 3 * head_width :],
        )
        return jnp.concatenate([query_grad, key_grad, value_grad], axis=1)

    results = lax.map(run_cluster, flat_rows).reshape(
        head_local, clus_here, cluster_width, 3 * head_width
    )
    back_spots = jnp.clip(run_starts[..., None] + slot_ids, 0, cluster_width - 1).reshape(
        head_local, clus_here, -1
    )
    outgoing = jnp.take_along_axis(results, back_spots[..., None], axis=2).reshape(
        head_local, clus_here, seq_count, capacity, 3 * head_width
    )
    outgoing, new_centroids = (jnp.transpose(outgoing, (2, 0, 1, 3, 4)), moved_cent)
    returned = lax.all_to_all(
        as_sent(outgoing), "seq", split_axis=0, concat_axis=0, tiled=True
    ).astype(outgoing.dtype)
    buffer_rows = jnp.zeros((heads_here * (tok_rows + 1), 3 * head_width), jnp.bfloat16)
    buffer_rows = buffer_rows.at[flat_index.reshape(-1)].set(returned.reshape(-1, 3 * head_width))
    grad_rows = buffer_rows.reshape(heads_here, tok_rows + 1, 3, head_width)[:, :tok_rows]
    grad_rows = jnp.transpose(grad_rows, (2, 1, 0, 3)).reshape(3, tok_rows, heads_here * head_width)
    partial_sum = jnp.einsum(
        "atc,adc->td", grad_rows, proj_weight, preferred_element_type=jnp.float32
    )
    input_grad = lax.psum_scatter(
        partial_sum.astype(jnp.bfloat16), "head", scatter_dimension=1, tiled=True
    )
    return (input_grad, new_centroids)


def solution(mesh):
    return jax.shard_map(
        shards,
        mesh=mesh,
        in_specs=(
            P("seq", "head"),
            P("seq", "head"),
            P("seq", "head"),
            P("seq", "head"),
            P("head", "seq", None),
            P("head", "seq", None),
            P(None, None, "head"),
        ),
        out_specs=(P("seq", "head"), P("head", "seq", None)),
        check_vma=False,
    )
```

profile of v0, /device:TPU:8, one launch (start us, length us, event | category | flops | bytes accessed | tf_op | source)
XLA Modules:
  0.0 546.2 jit_solution(6480575813026629535)
XLA Ops:
  7.2 0.9 copy.115
  8.1 52.3 %all_gather.3 = s32[2,32,1024]{2,0,1:T(2,128)S(1)} all-gather(s32[2,1,1024]{2,0,1:T(2,128)S(1)} %copy.115), channel_id=1, replica_groups=mesh['seq'=32,'head'=8] {'seq'}, dimensions={1}, use_global_device_ids=true | all-gather | bytes 270336 | tf_op jit(solution)/shard_map/all_gather | solution.py:86
  60.4 1.4 fusion.39
  62.1 39.9 %gather_fusion.1 = s32[4096]{0:T(1024)S(1)} fusion(s32[2,32,1024]{2,0,1:T(2,128)S(1)} %all_gather.3, s32[4096]{0:T(1024)S(1)} %reshape.712), kind=kCustom, calls=%fused_computation.1 | custom fusion | bytes 81920 | tf_op jit(solution)/shard_map/jit(take_along_axis)/gather | solution.py:91
  102.4 2.0 stack.15
  104.4 2.0 stack.16
  106.4 2.0 stack.17
  108.3 2.0 stack.18
  110.3 5.1 maximum_bitcast_fusion.1
  115.4 3.0 copy.124
  118.3 4.1 reshape.697
  122.5 3.1 concatenate.34
  125.6 3.4 reshape.698
  129.0 19.3 %gather_fusion = bf16[4096,512]{1,0:T(8,128)(2,1)} fusion(bf16[2050,512]{1,0:T(8,128)(2,1)} %reshape.698, s32[4096]{0:T(1024)S(1)} %broadcast_clamp_fusion), kind=kCustom, calls=%fused_computation | custom fusion | bytes 8404992 | tf_op jit(solution)/shard_map/jit(_take)/gather | solution.py:107
  148.2 3.9 broadcast_select_fusion
  152.1 6.6 %all-to-all-start = ((bf16[32,2,1,64,512]{4,3,1,2,0:T(8,128)(2,1)}), bf16[32,2,1,64,512]{4,3,1,2,0:T(8,128)(2,1)}, u32[]{:S(2)}, u32[]{:S(2)}) async-start(bf16[32,2,1,64,512]{4,3,1,2,0:T(8,128)(2,1)} %broadcast_select_fusion), calls=%async_computation | async-start | bytes 8388608 | tf_op jit(solution)/shard_map/all_to_all | solution.py:108
  158.9 0.4 reduce_window_sum.13
  159.5 17.6 %gather_fusion.2 = s32[2048]{0:T(1024)S(1)} fusion(s32[2,32]{1,0:T(2,128)S(1)} %bitcast.102, s32[2048]{0:T(1024)S(1)} %bitcast.105), kind=kCustom, calls=%fused_computation.2 | custom fusion | bytes 32768 | tf_op jit(solution)/shard_map/jit(take_along_axis)/gather | solution.py:119
  177.6 64.7 %all-to-all-done = bf16[32,2,1,64,512]{4,3,1,2,0:T(8,128)(2,1)} async-done(((bf16[32,2,1,64,512]{4,3,1,2,0:T(8,128)(2,1)}), bf16[32,2,1,64,512]{4,3,1,2,0:T(8,128)(2,1)}, u32[]{:S(2)}, u32[]{:S(2)}) %all-to-all-start) | async-done | bytes 4194336 | tf_op jit(solution)/shard_map/all_to_all | solution.py:108
  242.2 4.6 copy.127
  246.8 37.4 %gather_fusion.3 = bf16[2048,512]{1,0:T(8,128)(2,1)} fusion(bf16[2,2048,512]{2,1,0:T(8,128)(2,1)} %bitcast.106, s32[2048]{0:T(1024)S(1)} %bitcast.104), kind=kCustom, calls=%fused_computation.3 | custom fusion | bytes 4210688 | tf_op jit(solution)/shard_map/jit(take_along_axis)/gather | solution.py:120
  284.2 4.0 copy.128
  288.2 3.1 broadcast_select_fusion.1
  291.3 19.1 %while.19 = (s32[]{:T(128)}, bf16[2,1024,384]{2,1,0:T(8,128)(2,1)}, bf16[2,1024,512]{1,2,0:T(8,128)(2,1)}, s32[]{:T(128)}) while((s32[]{:T(128)}, bf16[2,1024,384]{2,1,0:T(8,128)(2,1)}, bf16[2,1024,512]{1,2,0:T(8,128)(2,1)}, s32[]{:T(128)}) %tuple.67), condition=%wide.region_12.13_spmd, body=%wide.region_5.12_spmd.sunk | while | flops 1222899200 | bytes 46174332 | solution.py:132
  291.3 1.3 dynamic-slice_bitcast_fusion.2
  292.6 0.4 fusion.130
  293.6 0.4 fusion.140
  294.9 0.6 fusion.134
  295.6 0.5 fusion.135
  296.1 0.5 fusion.136
  296.6 0.5 fusion.137
  297.0 0.5 fusion.138
  297.5 0.5 multiply_convert_fusion.2
  298.0 0.5 fusion.142
  298.5 0.4 fusion.143
  299.0 0.5 copy-done.1
  299.6 1.2 copy-done.2
  300.9 1.3 dynamic-slice_bitcast_fusion.2
  302.2 0.4 fusion.130
  303.2 0.4 fusion.140
  304.5 0.6 fusion.134
  305.1 0.5 fusion.135
  305.6 0.5 fusion.136
  306.1 0.5 fusion.137
  306.6 0.5 fusion.138
  307.1 0.5 multiply_convert_fusion.2
  307.6 0.5 fusion.142
  308.1 0.4 fusion.143
  308.5 0.5 copy-done.1
  309.2 1.2 copy-done.2
  310.4 72.9 %gather_fusion.4 = bf16[4096,384]{1,0:T(8,128)(2,1)} fusion(bf16[2,1024,384]{2,1,0:T(8,128)(2,1)} %get-tuple-element.131, s32[4096]{0:T(1024)S(1)} %bitcast.103), kind=kCustom, calls=%fused_computation.4 | custom fusion | bytes 6324224 | tf_op jit(solution)/shard_map/jit(take_along_axis)/gather | solution.py:138
  383.3 3.5 fusion.36
  386.8 8.8 %all-to-all-start.1 = ((bf16[32,2,1,64,384]{4,3,1,2,0:T(8,128)(2,1)}), bf16[32,2,1,64,384]{4,3,1,2,0:T(8,128)(2,1)}, u32[]{:S(2)}, u32[]{:S(2)}) async-start(bf16[32,2,1,64,384]{4,3,1,2,0:T(8,128)(2,1)} %fusion.36), calls=%async_computation.1 | async-start | bytes 6291456 | tf_op jit(solution)/shard_map/all_to_all | solution.py:142
  396.1 61.0 %all-to-all-done.1 = bf16[32,2,1,64,384]{4,3,1,2,0:T(8,128)(2,1)} async-done(((bf16[32,2,1,64,384]{4,3,1,2,0:T(8,128)(2,1)}), bf16[32,2,1,64,384]{4,3,1,2,0:T(8,128)(2,1)}, u32[]{:S(2)}, u32[]{:S(2)}) %all-to-all-start.1) | async-done | bytes 3145760 | tf_op jit(solution)/shard_map/all_to_all | solution.py:142
  457.1 19.8 %scatter_custom_fusion = bf16[2050,384]{1,0:T(8,128)(2,1)} fusion(s32[4096]{0:T(1024)S(1)} %bitcast.116, bf16[4096,384]{1,0:T(8,128)(2,1)} %bitcast.19, bf16[]{:T(256)} %constant.280.clone.1), kind=kCustom, calls=%fused_computation.67 | custom fusion | bytes 1574912 | tf_op jit(solution)/shard_map/scatter | solution.py:146
  476.8 3.7 copy.130
  480.5 5.1 reshape.702
  485.7 3.7 slice_bitcast_fusion
  489.3 6.2 %copy.131 = bf16[3,1024,2,128]{3,2,1,0:T(2,128)(2,1)} copy(bf16[3,1024,2,128]{1,2,3,0:T(2,128)(2,1)} %slice_bitcast_fusion) | data formatting | bytes 3145728 | tf_op jit(solution)/shard_map/transpose | solution.py:148
  495.5 3.7 reshape.703
  499.2 6.4 %bitcast_convert_fusion = bf16[1024,2048]{1,0:T(8,128)(2,1)} fusion(bf16[3,1024,256]{2,1,0:T(8,128)(2,1)} %reshape.703, bf16[3,2048,256]{2,1,0:T(8,128)(2,1)S(1)} %copy-done), kind=kOutput, calls=%fused_computation.59 | convolution fusion | flops 3223322624 | bytes 8912896 | tf_op jit(solution)/shard_map/atc,adc->td/dot_general | solution.py:149
  505.7 1.9 convert_reduce_fusion
  507.6 0.6 fusion.63
  508.2 31.2 %reduce-scatter.2.cloned.1.call-done = bf16[1024,256]{1,0:T(8,128)(2,1)} async-done(((bf16[1024,2048]{1,0:T(8,128)(2,1)}), bf16[1024,256]{1,0:T(8,128)(2,1)}) %reduce-scatter.2.cloned.1.call-update) | async-done | bytes 524304 | tf_op jit(solution)/shard_map/reduce_scatter | solution.py:152
  (66 shorter events, 5.4 us)
Async XLA Ops:
  7.2 492.1 %copy-start = (bf16[3,2048,256]{2,1,0:T(8,128)(2,1)S(1)}, bf16[3,2048,256]{2,1,0:T(8,128)(2,1)}, u32[]{:S(2)}) copy-start(bf16[3,2048,256]{2,1,0:T(8,128)(2,1)} %param.27) | copy-start | bytes 9437188
  152.1 6.6 %copy-start.3 = (s32[2,1,1024]{2,1,0:T(1,128)S(1)}, s32[2,1,1024]{2,1,0:T(1,128)}, u32[]{:S(2)}) copy-start(s32[2,1,1024]{2,1,0:T(1,128)} %param.25) | copy-start | bytes 24580
  152.1 90.1 %all-to-all-start = ((bf16[32,2,1,64,512]{4,3,1,2,0:T(8,128)(2,1)}), bf16[32,2,1,64,512]{4,3,1,2,0:T(8,128)(2,1)}, u32[]{:S(2)}, u32[]{:S(2)}) async-start(bf16[32,2,1,64,512]{4,3,1,2,0:T(8,128)(2,1)} %broadcast_select_fusion), calls=%async_computation | async-start | bytes 8388608 | tf_op jit(solution)/shard_map/all_to_all | solution.py:108
  298.0 1.4 copy-start.1
  299.6 1.2 copy-start.2
  307.6 1.4 copy-start.1
  309.2 1.2 copy-start.2
  386.8 70.3 %all-to-all-start.1 = ((bf16[32,2,1,64,384]{4,3,1,2,0:T(8,128)(2,1)}), bf16[32,2,1,64,384]{4,3,1,2,0:T(8,128)(2,1)}, u32[]{:S(2)}, u32[]{:S(2)}) async-start(bf16[32,2,1,64,384]{4,3,1,2,0:T(8,128)(2,1)} %fusion.36), calls=%async_computation.1 | async-start | bytes 6291456 | tf_op jit(solution)/shard_map/all_to_all | solution.py:142
  395.6 143.8 %reduce-scatter.2.cloned.1.call-start = ((), (), s32[]{:S(2)}) async-start(), calls=%async_computation.3 | async-start | bytes 4718592 | tf_op jit(solution)/shard_map/reduce_scatter | solution.py:152
  505.7 1.9 copy-start.4
Sparse Core Ops, SparseCore 0:
  505.8 33.5 reduce-scatter.1
where the time goes:
time: 553 us; the launch traced here: 546 us
  local copies, waits for them, and re-layouts  267 us (48%)
  waiting for transfers between devices  157 us (28%)
  blocking collectives  52.3 us (9%)
  other arithmetic  23.8 us (4%)
  matrix products  16.2 us (3%)
  starting transfers between devices  15.7 us (3%)
  between operations  14.3 us (3%)
    gather x1, local copies, waits for them, and re-layouts, shards(): jnp.take_along_axis(results, back_spots[..., None], axis=2)  72.9 us
    all_to_all x1, waiting for transfers between devices, shards(): lax.all_to_all(payload, 'seq', split_axis=0, concat_axis=0, tiled=True)  64.7 us
    all_to_all x1, waiting for transfers between devices, shards(): lax.all_to_all(as_sent(outgoing), 'seq', split_axis=0, concat_axis=0, til...  61 us
    all_gather x1, blocking collectives, shards(): everything = lax.all_gather(members, 'seq', axis=1, tiled=True)  52.3 us
    gather x2, local copies, waits for them, and re-layouts, shards(): jnp.take_along_axis(pooled, (source_of * capacity + offset)[..., None], a...  41.3 us
    gather x3, local copies, waits for them, and re-layouts, shards(): jnp.take_along_axis(everything, jnp.clip(spots, 0, cluster_width - 1), ax...  40 us
    reduce_scatter x1, waiting for transfers between devices, shards(): lax.psum_scatter(partial_sum.astype(jnp.bfloat16), 'head', scatter_dimens...  31.2 us
    scatter x2, local copies, waits for them, and re-layouts, shards(): buffer_rows.at[flat_index.reshape(-1)]  23.5 us
  transfers between devices with their start and end apart: 3, of which 3 were waited for; matrix products, arithmetic and copies ran while one was open for 4% of the time, Pallas kernels for 0%

commit v1 on v0

v1 whole, which is shorter than its diff:
```python
import math

import jax
import jax.numpy as jnp
from jax import lax
from jax.experimental import pallas as pl
from jax.experimental.pallas import tpu as pltpu
from jax.sharding import PartitionSpec as P

MESH = pl.DeviceIdType.MESH
F32 = jnp.float32
BF16 = jnp.bfloat16

decay_rate = 0.99

N = 32
NZ, NX = 8, 4
NY = 4
TOK = 1024
W = 1024
CAP = 64
HD = 128
HEADS = 2
SLOTS = N * CAP
GROUP = 4
BLK = 256
RC = 8
RROWS = TOK // RC
SELF_STEP = (NZ - 1) * NX


def one_hot(mask):
    return jnp.where(mask, 1.0, 0.0).astype(BF16)


def iota(shape, dim):
    return lax.broadcasted_iota(jnp.int32, shape, dim).astype(F32)


def dot_nt(a, b):
    return lax.dot_general(a, b, (((1,), (1,)), ((), ())), preferred_element_type=F32)


def dot_nn(a, b):
    return jnp.dot(a, b, preferred_element_type=F32)


def kernel(
    q_ref, k_ref, v_ref, g_ref, mem_ref, cent_ref, w_ref,
    out_ref, newc_ref,
    tab, codes_s, codes_r, destrow, dest_t, slot_t, hot,
    stage_f, recv_f, x_ref, y_ref, dk_ref, dv_ref, p_scr, d_scr, k_t,
    stage_r, recv_r, z_ref, part, part_r, p2, hop_r, hop_s, dir_r, last_r,
    code_ss, code_rs, fwd_ss, fwd_rs, ret_ss, ret_rs, self_sem,
    core_ss, core_rs, hop_ss, hop_rs, dir_ss, dir_rs, last_ss, last_rs,
):
    me = lax.axis_index("seq")
    hd = lax.axis_index("head")
    my_z, my_x = lax.div(me, NX), lax.rem(me, NX)
    my_y, core = lax.div(hd, 2), lax.rem(hd, 2)
    sibling = my_y * 2 + (1 - core)
    y_next = lax.rem(my_y + 1, NY)
    y_prev = lax.rem(my_y + NY - 1, NY)
    y_far = lax.rem(my_y + 2, NY)
    next_hd = y_next * 2 + core
    prev_hd = y_prev * 2 + core

    def peer(n):
        step = lax.div(n, NX)
        dx = lax.rem(n, NX)
        half = lax.div(step, 2)
        odd = lax.rem(step, 2)
        dz = jnp.where(step == NZ - 1, 0, jnp.where(odd == 1, NZ - 1 - half, 1 + half))
        return lax.rem(my_z + dz, NZ) * NX + lax.rem(my_x + dx, NX)

    barrier = pltpu.get_barrier_semaphore()

    def greet(n, carry):
        @pl.when(n != SELF_STEP)
        def _():
            pl.semaphore_signal(barrier, inc=1, device_id=(peer(n), hd), device_id_type=MESH)
        return carry

    lax.fori_loop(0, N, greet, 0)
    for other in (sibling, next_hd, prev_hd):
        pl.semaphore_signal(barrier, inc=1, device_id=(me, other), device_id_type=MESH)

    for h in range(HEADS):
        m = mem_ref[h]
        hi = m >> 10
        lo = m & (TOK - 1)
        dev = lax.broadcasted_iota(jnp.int32, (N, W), 0)
        eq = hi == dev
        start = jnp.sum(jnp.where(hi < dev, 1.0, 0.0), axis=1, keepdims=True)
        count = jnp.sum(jnp.where(eq, 1.0, 0.0), axis=1, keepdims=True)
        start_of = jnp.sum(jnp.where(eq, start, 0.0), axis=0, keepdims=True)
        rank = iota((1, W), 1) + 1.0 - start_of
        ranks = jnp.where(eq, rank, 0.0).astype(BF16)
        for tb in range(TOK // BLK):
            tok = lax.broadcasted_iota(jnp.int32, (BLK, W), 0) + tb * BLK
            codes = dot_nt(ranks, one_hot(lo == tok))
            for part_at in range(BLK // 128):
                codes_s[:, h, tb * (BLK // 128) + part_at, :] = codes[
                    :, part_at * 128 : (part_at + 1) * 128
                ]
        slot = lax.broadcasted_iota(jnp.int32, (N, SLOTS), 1)
        dev2 = lax.broadcasted_iota(jnp.int32, (N, SLOTS), 0)
        rank_at = (slot & (CAP - 1)).astype(F32)
        place = jnp.where(rank_at < count, start + rank_at, -1.0)
        dest = jnp.sum(jnp.where((slot >> 6) == dev2, place, 0.0), axis=0, keepdims=True)
        destrow[h] = dest
        dest_t[h] = jnp.transpose(jnp.broadcast_to(dest, (128, SLOTS)))

    pl.semaphore_wait(barrier, N - 1 + 3)

    def code_copy(n, src_at, dst_at, other):
        return pltpu.make_async_remote_copy(
            src_ref=codes_s.at[src_at], dst_ref=codes_r.at[dst_at],
            send_sem=code_ss.at[n], recv_sem=code_rs.at[dst_at],
            device_id=(other, hd), device_id_type=MESH,
        )

    def send_codes(n, carry):
        @pl.when(n != SELF_STEP)
        def _():
            to = peer(n)
            code_copy(n, to, me, to).start()
        return carry

    lax.fori_loop(0, N, send_codes, 0)
    codes_r[me] = codes_s[me]
    for h in range(HEADS):
        for at, ref in enumerate((q_ref, k_ref, v_ref, g_ref)):
            tab[h, :, at * HD : (at + 1) * HD] = ref[:, h * HD : (h + 1) * HD]

    def wait_codes(n, carry):
        @pl.when(n != SELF_STEP)
        def _():
            src = peer(n)
            code_copy(n, src, src, src).wait_recv()
        return carry

    lax.fori_loop(0, N, wait_codes, 0)

    def fwd_copy(h, n, dst_at, other):
        return pltpu.make_async_remote_copy(
            src_ref=stage_f.at[h, n], dst_ref=recv_f.at[h, dst_at],
            send_sem=fwd_ss.at[h, n], recv_sem=fwd_rs.at[h, dst_at],
            device_id=(other, hd), device_id_type=MESH,
        )

    def ret_copy(h, n, dst_at, other):
        return pltpu.make_async_remote_copy(
            src_ref=stage_r.at[h, n], dst_ref=recv_r.at[h, dst_at],
            send_sem=ret_ss.at[h, n], recv_sem=ret_rs.at[h, dst_at],
            device_id=(other, hd), device_id_type=MESH,
        )

    def fwd_self(h):
        return pltpu.make_async_copy(stage_f.at[h, SELF_STEP], recv_f.at[h, me], self_sem.at[0, h])

    def ret_self(h):
        return pltpu.make_async_copy(stage_r.at[h, SELF_STEP], recv_r.at[h, me], self_sem.at[1, h])

    def launch(h, gi, copy_of, self_of):
        for u in range(GROUP):
            n = gi * GROUP + u
            to = peer(n)

            @pl.when(n != SELF_STEP)
            def _():
                copy_of(h, n, me, to).start()

            @pl.when(n == SELF_STEP)
            def _():
                self_of(h).start()

    def wait_all(h, copy_of, self_of):
        def one(n, carry):
            @pl.when(n != SELF_STEP)
            def _():
                src = peer(n)
                copy_of(h, n, src, src).wait_recv()
            return carry

        lax.fori_loop(0, N, one, 0)
        self_of(h).wait()

    rank_rows = iota((CAP, 128), 0) + 1.0
    lanes = iota((CAP, 128), 1)

    def gather_head(h, carry):
        def group(gi, inner):
            for u in range(GROUP):
                to = peer(gi * GROUP + u)
                for tc in range(TOK // 128):
                    row = codes_r[to, h, tc : tc + 1, :]
                    hot[u * CAP : (u + 1) * CAP, tc * 128 : (tc + 1) * 128] = one_hot(row == rank_rows)
            rows = dot_nn(hot[:, :TOK], tab[h])
            stage_f[h, pl.ds(gi * GROUP, GROUP)] = rows.astype(BF16).reshape(GROUP, CAP, 4 * HD)
            launch(h, gi, fwd_copy, fwd_self)
            return inner

        return lax.fori_loop(0, N // GROUP, group, carry)

    lax.fori_loop(0, HEADS, gather_head, 0)

    for h in range(HEADS):
        slot = jnp.zeros((TOK // 128, 128), F32)
        for c in range(N):
            code = codes_r[c, h]
            slot = slot + jnp.where(code > 0.0, code + (c * CAP - 1.0), 0.0)
        for tc in range(TOK // 128):
            slot_t[h, tc * 128 : (tc + 1) * 128, :] = jnp.transpose(
                jnp.broadcast_to(slot[tc : tc + 1, :], (128, 128))
            )

    exp_scale = math.log2(math.e) / math.sqrt(HD)
    scale = 1.0 / math.sqrt(HD)
    causal = lax.broadcasted_iota(jnp.int32, (BLK, BLK), 0) <= lax.broadcasted_iota(
        jnp.int32, (BLK, BLK), 1
    )

    def cluster_head(h, carry):
        wait_all(h, fwd_copy, fwd_self)

        def order(ib, sums):
            place = iota((BLK, 128), 0) + (ib * BLK).astype(F32)
            for pc in range(SLOTS // 128):
                row = destrow[h, :, pc * 128 : (pc + 1) * 128]
                hot[:, pc * 128 : (pc + 1) * 128] = one_hot(row == place)
            rows = dot_nn(hot[...], recv_f[h].reshape(SLOTS, 4 * HD))
            x_ref[pl.ds(ib * BLK, BLK), :] = rows.astype(BF16)
            return sums + jnp.sum(rows[:, :HD] + rows[:, HD : 2 * HD], axis=0, keepdims=True)

        sums = lax.fori_loop(0, W // BLK, order, jnp.zeros((1, HD), F32))
        newc_ref[h] = decay_rate * cent_ref[h] + 0.5 * (1.0 - decay_rate) * sums

        k_t[...] = jnp.transpose(x_ref[:, HD : 2 * HD].astype(F32)).astype(BF16)

        for b in range(W // BLK):
            low = b * BLK
            q_b = x_ref[low : low + BLK, 0:HD]
            g_b = x_ref[low : low + BLK, 3 * HD : 4 * HD]
            top = None
            for jb in range(b + 1):
                s = dot_nt(x_ref[jb * BLK : (jb + 1) * BLK, HD : 2 * HD], q_b)
                if jb == b:
                    s = jnp.where(causal, s, -jnp.inf)
                p_scr[jb] = s
                part_top = jnp.max(s, axis=0, keepdims=True)
                top = part_top if top is None else jnp.maximum(top, part_top)
            total = jnp.zeros((1, BLK), F32)
            delta = jnp.zeros((1, BLK), F32)
            for jb in range(b + 1):
                p = jnp.exp2((p_scr[jb] - top) * exp_scale)
                d = dot_nt(x_ref[jb * BLK : (jb + 1) * BLK, 2 * HD : 3 * HD], g_b)
                p_scr[jb] = p
                d_scr[jb] = d
                total = total + jnp.sum(p, axis=0, keepdims=True)
                delta = delta + jnp.sum(p * d, axis=0, keepdims=True)
            inv = 1.0 / total
            delta = delta * inv
            dq_t = jnp.zeros((HD, BLK), F32)
            for jb in range(b + 1):
                rows = slice(jb * BLK, (jb + 1) * BLK)
                p = p_scr[jb] * inv
                p_low = p.astype(BF16)
                ds = (p * (d_scr[jb] - delta)).astype(BF16)
                dv = dot_nn(p_low, g_b)
                dk = dot_nn(ds, q_b)
                dq_t = dq_t + dot_nn(k_t[:, rows], ds)
                if jb == b:
                    dv_ref[rows, :] = dv
                    dk_ref[rows, :] = dk
                else:
                    dv_ref[rows, :] += dv
                    dk_ref[rows, :] += dk
            y_ref[low : low + BLK, 0:HD] = (jnp.transpose(dq_t) * scale).astype(BF16)
        y_ref[:, HD : 2 * HD] = (dk_ref[...] * scale).astype(BF16)
        y_ref[:, 2 * HD : 3 * HD] = dv_ref[...].astype(BF16)

        def group(gi, inner):
            for u in range(GROUP):
                to = peer(gi * GROUP + u)
                place = dest_t[h, pl.ds(pl.multiple_of(to * CAP, CAP), CAP), :]
                for ic in range(W // 128):
                    hot[u * CAP : (u + 1) * CAP, ic * 128 : (ic + 1) * 128] = one_hot(
                        place == lanes + ic * 128.0
                    )
            rows = dot_nn(hot[:, :W], y_ref[...])
            stage_r[h, pl.ds(gi * GROUP, GROUP)] = rows.astype(BF16).reshape(GROUP, CAP, 3 * HD)
            launch(h, gi, ret_copy, ret_self)
            return inner

        return lax.fori_loop(0, N // GROUP, group, carry)

    lax.fori_loop(0, HEADS, cluster_head, 0)

    def tokens(h, tb):
        wide = iota((BLK, 128), 1)
        rows_at = pl.ds(pl.multiple_of(tb * BLK, BLK), BLK)
        place = slot_t[h, rows_at, :]
        for pc in range(SLOTS // 128):
            hot[:, pc * 128 : (pc + 1) * 128] = one_hot(place == wide + pc * 128.0)
        rows = dot_nn(hot[...], recv_r[h].reshape(SLOTS, 3 * HD)).astype(BF16)
        for a in range(3):
            at = a * HEADS * HD + h * HD
            z_ref[rows_at, at : at + HD] = rows[:, a * HD : (a + 1) * HD]

    wait_all(0, ret_copy, ret_self)
    lax.fori_loop(0, TOK // BLK, lambda tb, c: (tokens(0, tb), c)[1], 0)
    wait_all(1, ret_copy, ret_self)

    def core_copy(rc):
        return pltpu.make_async_remote_copy(
            src_ref=part.at[rc, 1 - core], dst_ref=part_r.at[rc],
            send_sem=core_ss.at[rc], recv_sem=core_rs.at[rc],
            device_id=(me, sibling), device_id_type=MESH,
        )

    def hop_copy(rc):
        return pltpu.make_async_remote_copy(
            src_ref=p2.at[rc, y_far], dst_ref=hop_r.at[rc],
            send_sem=hop_ss.at[rc], recv_sem=hop_rs.at[rc],
            device_id=(me, next_hd if rc % 2 == 0 else prev_hd), device_id_type=MESH,
        )

    def dir_copy(rc):
        return pltpu.make_async_remote_copy(
            src_ref=p2.at[rc, y_prev if rc % 2 == 0 else y_next], dst_ref=dir_r.at[rc],
            send_sem=dir_ss.at[rc], recv_sem=dir_rs.at[rc],
            device_id=(me, prev_hd if rc % 2 == 0 else next_hd), device_id_type=MESH,
        )

    def last_copy(rc):
        return pltpu.make_async_remote_copy(
            src_ref=hop_s.at[rc], dst_ref=last_r.at[rc],
            send_sem=last_ss.at[rc], recv_sem=last_rs.at[rc],
            device_id=(me, next_hd if rc % 2 == 0 else prev_hd), device_id_type=MESH,
        )

    def project(tb):
        tokens(1, tb)
        z = z_ref[tb * BLK : (tb + 1) * BLK, :]

        def one(d, carry):
            acc = None
            for a in range(3):
                term = dot_nt(
                    z[:, a * HEADS * HD : (a + 1) * HEADS * HD],
                    w_ref[a, pl.ds(pl.multiple_of(d * 256, 256), 256), :],
                )
                acc = term if acc is None else acc + term
            low = acc.astype(BF16)
            for piece in range(BLK // RROWS):
                part[tb * (BLK // RROWS) + piece, lax.rem(d, 2), lax.div(d, 2)] = low[
                    piece * RROWS : (piece + 1) * RROWS
                ]
            return carry

        lax.fori_loop(0, 2 * NY, one, 0)

    def merge(rc):
        core_copy(rc).wait_recv()
        p2[rc] = (part[rc, core].astype(F32) + part_r[rc].astype(F32)).astype(BF16)
        hop_copy(rc).start()
        dir_copy(rc).start()

    def relay(rc):
        hop_copy(rc).wait_recv()
        mine = p2[rc, y_next if rc % 2 == 0 else y_prev]
        hop_s[rc] = (hop_r[rc].astype(F32) + mine.astype(F32)).astype(BF16)
        last_copy(rc).start()

    def finish(rc):
        dir_copy(rc).wait_recv()
        last_copy(rc).wait_recv()
        total = p2[rc, my_y].astype(F32) + dir_r[rc].astype(F32) + last_r[rc].astype(F32)
        out_ref[rc * RROWS : (rc + 1) * RROWS, :] = total.astype(BF16)

    per = BLK // RROWS
    for step in range(TOK // BLK + 3):
        if step < TOK // BLK:
            project(step)
            for rc in range(step * per, (step + 1) * per):
                core_copy(rc).start()
        if 1 <= step <= TOK // BLK:
            for rc in range((step - 1) * per, step * per):
                merge(rc)
        if 2 <= step <= TOK // BLK + 1:
            for rc in range((step - 2) * per, (step - 1) * per):
                relay(rc)
    for rc in range(RC):
        finish(rc)

    def drain(n, carry):
        @pl.when(n != SELF_STEP)
        def _():
            to = peer(n)
            code_copy(n, to, me, to).wait_send()
            for h in range(HEADS):
                fwd_copy(h, n, me, to).wait_send()
                ret_copy(h, n, me, to).wait_send()
        return carry

    lax.fori_loop(0, N, drain, 0)
    for rc in range(RC):
        core_copy(rc).wait_send()
        hop_copy(rc).wait_send()
        dir_copy(rc).wait_send()
        last_copy(rc).wait_send()


def shards(queries, keys, values, out_grad, members, centroids, proj_weight):
    vmem = pl.BlockSpec(memory_space=pltpu.VMEM)
    dma = pltpu.SemaphoreType.DMA
    return pl.pallas_call(
        kernel,
        out_shape=(
            jax.ShapeDtypeStruct((TOK, HEADS * HD), BF16),
            jax.ShapeDtypeStruct((HEADS, 1, HD), F32),
        ),
        in_specs=[vmem] * 7,
        out_specs=(vmem, vmem),
        scratch_shapes=[
            pltpu.VMEM((HEADS, TOK, 4 * HD), BF16),
            pltpu.VMEM((N, HEADS, TOK // 128, 128), F32),
            pltpu.VMEM((N, HEADS, TOK // 128, 128), F32),
            pltpu.VMEM((HEADS, 1, SLOTS), F32),
            pltpu.VMEM((HEADS, SLOTS, 128), F32),
            pltpu.VMEM((HEADS, TOK, 128), F32),
            pltpu.VMEM((BLK, SLOTS), BF16),
            pltpu.VMEM((HEADS, N, CAP, 4 * HD), BF16),
            pltpu.VMEM((HEADS, N, CAP, 4 * HD), BF16),
            pltpu.VMEM((W, 4 * HD), BF16),
            pltpu.VMEM((W, 3 * HD), BF16),
            pltpu.VMEM((W, HD), F32),
            pltpu.VMEM((W, HD), F32),
            pltpu.VMEM((W // BLK, BLK, BLK), F32),
            pltpu.VMEM((W // BLK, BLK, BLK), F32),
            pltpu.VMEM((HD, W), BF16),
            pltpu.VMEM((HEADS, N, CAP, 3 * HD), BF16),
            pltpu.VMEM((HEADS, N, CAP, 3 * HD), BF16),
            pltpu.VMEM((TOK, 3 * HEADS * HD), BF16),
            pltpu.VMEM((RC, 2, NY, RROWS, 256), BF16),
            pltpu.VMEM((RC, NY, RROWS, 256), BF16),
            pltpu.VMEM((RC, NY, RROWS, 256), BF16),
            pltpu.VMEM((RC, RROWS, 256), BF16),
            pltpu.VMEM((RC, RROWS, 256), BF16),
            pltpu.VMEM((RC, RROWS, 256), BF16),
            pltpu.VMEM((RC, RROWS, 256), BF16),
            dma((N,)), dma((N,)),
            dma((HEADS, N)), dma((HEADS, N)),
            dma((HEADS, N)), dma((HEADS, N)),
            dma((2, HEADS)),
            dma((RC,)), dma((RC,)),
            dma((RC,)), dma((RC,)),
            dma((RC,)), dma((RC,)),
            dma((RC,)), dma((RC,)),
        ],
        compiler_params=pltpu.CompilerParams(
            collective_id=0, has_side_effects=True, vmem_limit_bytes=60 * 1024 * 1024
        ),
    )(queries, keys, values, out_grad, members, centroids, proj_weight)


def solution(mesh):
    return jax.shard_map(
        shards,
        mesh=mesh,
        in_specs=(
            P("seq", "head"),
            P("seq", "head"),
            P("seq", "head"),
            P("seq", "head"),
            P("head", "seq", None),
            P("head", "seq", None),
            P(None, None, "head"),
        ),
        out_specs=(P("seq", "head"), P("head", "seq", None)),
        check_vma=False,
    )
```

time: 553 us -> 219 us (0.40); the launches traced: 546 us -> 219 us
  local copies, waits for them, and re-layouts: 267 us -> 3.07 us
  Pallas kernels: 0 us -> 215 us
  waiting for transfers between devices: 157 us -> 0 us
  blocking collectives: 52.3 us -> 0 us
  other arithmetic: 23.8 us -> 0 us
  matrix products: 16.2 us -> 0 us
  starting transfers between devices: 15.7 us -> 0 us
  between operations: 14.3 us -> 0.64 us
    pallas_call x0 -> x1, Pallas kernels: none -> 215 us  [shards(): pl.pallas_call(kernel, out_shape=(jax.ShapeDtypeStruct((TOK, HEADS * HD),...]
    gather x10 -> x0, local copies, waits for them, and re-layouts: 191 us -> none  [the longest x1 72.9 us: shards(): jnp.take_along_axis(results, back_spots[..., None], axis=2)]
    all_to_all x2 -> x0, waiting for transfers between devices: 126 us -> none  [the longest x1 64.7 us: shards(): lax.all_to_all(payload, 'seq', split_axis=0, concat_axis=0, tiled=True)]
    all_gather x1 -> x0, blocking collectives: 52.3 us -> none  [shards(): everything = lax.all_gather(members, 'seq', axis=1, tiled=True)]
    reduce_scatter x1 -> x0, waiting for transfers between devices: 31.2 us -> none  [shards(): lax.psum_scatter(partial_sum.astype(jnp.bfloat16), 'head', scatter_dimens...]
    scatter x2 -> x0, local copies, waits for them, and re-layouts: 23.5 us -> none  [shards(): buffer_rows.at[flat_index.reshape(-1)]]
    reshape x5 -> x0, local copies, waits for them, and re-layouts: 16.5 us -> none  [the longest x1 5.11 us: shards(): buffer_rows.reshape(heads_here, tok_rows + 1, 3, head_width)[:, :tok_rows]]
    dot_general x25 -> x0, matrix products: 16.2 us -> none  [the longest x1 6.44 us: shards(): jnp.einsum('atc,adc->td', grad_rows, proj_weight, preferred_element_type=...]
  transfers between devices with their start and end apart: 3 -> 0, of which waited for: 3 -> 0; matrix products, arithmetic and copies ran while one was open for 4% -> 0% of each run, Pallas kernels for 0% -> 0%
where the time goes in v1:
time: 219 us
  Pallas kernels  215 us (98%)
  local copies, waits for them, and re-layouts  3.07 us (1%)
    pallas_call x1, Pallas kernels, shards(): pl.pallas_call(kernel, out_shape=(jax.ShapeDtypeStruct((TOK, HEADS * HD),...  215 us

profile of v1, /device:TPU:8, one launch (start us, length us, event | category | flops | bytes accessed | tf_op | source)
XLA Modules:
  0.0 218.7 jit_solution(11760391709191941349)
XLA Ops:
  0.6 214.9 %shard_map.86 = (bf16[1024,256]{1,0:T(8,128)(2,1)}, f32[2,1,128]{2,1,0:T(1,128)}) custom-call(bf16[1024,256]{1,0:T(8,128)(2,1)} %q_ref.1, bf16[1024,256]{1,0:T(8,128)(2,1)} %k_ref.1, bf16[1024,256]{1,0:T(8,128)(2,1)} %v_ref.1, bf16[1024,256]{1,0:T(8,128)(2,1)} %g_ref.1, s32[2,1,1024]{2,1,0:T(1,128)} %mem_ref.1, f32[2,1,128]{2,1,0:T(1,128)} %cent_ref.1, ...), custom_call_target="tpu_custom_call" | custom-call | tf_op jit(solution)/shard_map/pallas_call | solution.py:418
  215.6 1.9 copy.11
  217.5 1.2 copy.12

commit v2 on v1

--- a/solution.py
+++ b/solution.py
@@ -26,6 +26,7 @@
 BLK = 256
 RC = 8
 RROWS = TOK // RC
+TILES = TOK // 128
 SELF_STEP = (NZ - 1) * NX
 
 
@@ -46,11 +47,11 @@
 
 
 def kernel(
-    q_ref, k_ref, v_ref, g_ref, mem_ref, cent_ref, w_ref,
+    q_hbm, k_hbm, v_hbm, g_hbm, mem_hbm, cent_hbm, w_hbm,
     out_ref, newc_ref,
-    tab, codes_s, codes_r, destrow, dest_t, slot_t, hot,
+    mem_ref, cent_ref, w_ref, in_sem, codes_w, tab, codes_s, codes_r, destrow, dest_t, slot_t, hot,
     stage_f, recv_f, x_ref, y_ref, dk_ref, dv_ref, p_scr, d_scr, k_t,
-    stage_r, recv_r, z_ref, part, part_r, p2, hop_r, hop_s, dir_r, last_r,
+    stage_r, recv_r, first, part, part_r, p2, hop_r, hop_s, dir_r, last_r,
     code_ss, code_rs, fwd_ss, fwd_rs, ret_ss, ret_rs, self_sem,
     core_ss, core_rs, hop_ss, hop_rs, dir_ss, dir_rs, last_ss, last_rs,
 ):
@@ -85,74 +86,84 @@
     for other in (sibling, next_hd, prev_hd):
         pl.semaphore_signal(barrier, inc=1, device_id=(me, other), device_id_type=MESH)
 
+    mem_in = pltpu.make_async_copy(mem_hbm, mem_ref, in_sem.at[0])
+    mem_in.start()
+    cent_in = pltpu.make_async_copy(cent_hbm, cent_ref, in_sem.at[1])
+    cent_in.start()
+    for h in range(HEADS):
+        for at, ref in enumerate((q_hbm, k_hbm, v_hbm, g_hbm)):
+            pltpu.make_async_copy(
+                ref.at[:, h * HD : (h + 1) * HD], tab.at[h, :, at * HD : (at + 1) * HD], in_sem.at[2]
+            ).start()
+    for h in range(HEADS):
+        for a in range(3):
+            pltpu.make_async_copy(
+                w_hbm.at[a, :, h * HD : (h + 1) * HD], w_ref.at[h, :, a * HD : (a + 1) * HD], in_sem.at[3]
+            ).start()
+    mem_in.wait()
+
+    runs = []
     for h in range(HEADS):
         m = mem_ref[h]
-        hi = m >> 10
-        lo = m & (TOK - 1)
         dev = lax.broadcasted_iota(jnp.int32, (N, W), 0)
-        eq = hi == dev
-        start = jnp.sum(jnp.where(hi < dev, 1.0, 0.0), axis=1, keepdims=True)
+        eq = (m >> 10) == dev
+        start = jnp.sum(jnp.where((m >> 10) < dev, 1.0, 0.0), axis=1, keepdims=True)
         count = jnp.sum(jnp.where(eq, 1.0, 0.0), axis=1, keepdims=True)
         start_of = jnp.sum(jnp.where(eq, start, 0.0), axis=0, keepdims=True)
         rank = iota((1, W), 1) + 1.0 - start_of
-        ranks = jnp.where(eq, rank, 0.0).astype(BF16)
-        for tb in range(TOK // BLK):
-            tok = lax.broadcasted_iota(jnp.int32, (BLK, W), 0) + tb * BLK
-            codes = dot_nt(ranks, one_hot(lo == tok))
-            for part_at in range(BLK // 128):
-                codes_s[:, h, tb * (BLK // 128) + part_at, :] = codes[
-                    :, part_at * 128 : (part_at + 1) * 128
-                ]
+        runs.append((start, count))
+        ranks = jnp.where(
+            (m >> 7) == lax.broadcasted_iota(jnp.int32, (N * TILES, W), 0), rank, 0.0
+        ).astype(BF16)
+        low = one_hot((m & 127) == lax.broadcasted_iota(jnp.int32, (128, W), 0))
+        codes_w[:, h] = dot_nt(ranks, low).reshape(N, TILES, 128)
+    codes_s[...] = codes_w[...].reshape(N, HEADS * TILES, 128).astype(BF16)
+
+    pl.semaphore_wait(barrier, N - 1 + 3)
+
+    def code_copy(src, dst, step, other):
+        return pltpu.make_async_remote_copy(
+            src_ref=src, dst_ref=dst, send_sem=code_ss.at[0], recv_sem=code_rs.at[step],
+            device_id=(other, hd), device_id_type=MESH,
+        )
+
+    def send_codes(n, carry):
+        @pl.when(n != SELF_STEP)
+        def _():
+            to = peer(n)
+            step = lax.div(n, NX)
+            swap = step + 1 - 2 * lax.rem(step, 2)
+            there = jnp.where(step < NZ - 2, swap, step)
+            code_copy(codes_s.at[to], codes_r.at[me], there, to).start()
+        return carry
+
+    def wait_codes(step, count):
+        some = pl.ds(0, count)
+        code_copy(codes_s.at[some], codes_r.at[some], step, me).wait_recv()
+
+    lax.fori_loop(0, N, send_codes, 0)
+    codes_r[me] = codes_s[me]
+
+    for h in range(HEADS):
+        start, count = runs[h]
         slot = lax.broadcasted_iota(jnp.int32, (N, SLOTS), 1)
         dev2 = lax.broadcasted_iota(jnp.int32, (N, SLOTS), 0)
         rank_at = (slot & (CAP - 1)).astype(F32)
         place = jnp.where(rank_at < count, start + rank_at, -1.0)
-        dest = jnp.sum(jnp.where((slot >> 6) == dev2, place, 0.0), axis=0, keepdims=True)
-        destrow[h] = dest
-        dest_t[h] = jnp.transpose(jnp.broadcast_to(dest, (128, SLOTS)))
-
-    pl.semaphore_wait(barrier, N - 1 + 3)
-
-    def code_copy(n, src_at, dst_at, other):
+        destrow[h] = jnp.sum(jnp.where((slot >> 6) == dev2, place, 0.0), axis=0, keepdims=True)
+    pltpu.make_async_copy(tab, tab, in_sem.at[2]).wait()
+
+    def fwd_copy(h, src, dst, other):
         return pltpu.make_async_remote_copy(
-            src_ref=codes_s.at[src_at], dst_ref=codes_r.at[dst_at],
-            send_sem=code_ss.at[n], recv_sem=code_rs.at[dst_at],
+            src_ref=stage_f.at[h, src], dst_ref=recv_f.at[h, dst],
+            send_sem=fwd_ss.at[h], recv_sem=fwd_rs.at[h],
             device_id=(other, hd), device_id_type=MESH,
         )
 
-    def send_codes(n, carry):
-        @pl.when(n != SELF_STEP)
-        def _():
-            to = peer(n)
-            code_copy(n, to, me, to).start()
-        return carry
-
-    lax.fori_loop(0, N, send_codes, 0)
-    codes_r[me] = codes_s[me]
-    for h in range(HEADS):
-        for at, ref in enumerate((q_ref, k_ref, v_ref, g_ref)):
-            tab[h, :, at * HD : (at + 1) * HD] = ref[:, h * HD : (h + 1) * HD]
-
-    def wait_codes(n, carry):
-        @pl.when(n != SELF_STEP)
-        def _():
-            src = peer(n)
-            code_copy(n, src, src, src).wait_recv()
-        return carry
-
-    lax.fori_loop(0, N, wait_codes, 0)
-
-    def fwd_copy(h, n, dst_at, other):
+    def ret_copy(h, src, dst, other):
         return pltpu.make_async_remote_copy(
-            src_ref=stage_f.at[h, n], dst_ref=recv_f.at[h, dst_at],
-            send_sem=fwd_ss.at[h, n], recv_sem=fwd_rs.at[h, dst_at],
-            device_id=(other, hd), device_id_type=MESH,
-        )
-
-    def ret_copy(h, n, dst_at, other):
-        return pltpu.make_async_remote_copy(
-            src_ref=stage_r.at[h, n], dst_ref=recv_r.at[h, dst_at],
-            send_sem=ret_ss.at[h, n], recv_sem=ret_rs.at[h, dst_at],
+            src_ref=stage_r.at[h, src], dst_ref=recv_r.at[h, dst],
+            send_sem=ret_ss.at[h], recv_sem=ret_rs.at[h],
             device_id=(other, hd), device_id_type=MESH,
         )
 
@@ -175,15 +186,10 @@
             def _():
                 self_of(h).start()
 
+    others = pl.ds(0, N - 1)
+
     def wait_all(h, copy_of, self_of):
-        def one(n, carry):
-            @pl.when(n != SELF_STEP)
-            def _():
-                src = peer(n)
-                copy_of(h, n, src, src).wait_recv()
-            return carry
-
-        lax.fori_loop(0, N, one, 0)
+        copy_of(h, others, others, me).wait_recv()
         self_of(h).wait()
 
     rank_rows = iota((CAP, 128), 0) + 1.0
@@ -191,10 +197,23 @@
 
     def gather_head(h, carry):
         def group(gi, inner):
+            @pl.when((h == 0) & (gi < NZ - 1))
+            def _():
+                wait_codes(gi, NX)
+
+            @pl.when((h == 0) & (gi == NZ - 1))
+            def _():
+                wait_codes(gi, NX - 1)
+
             for u in range(GROUP):
                 to = peer(gi * GROUP + u)
-                for tc in range(TOK // 128):
-                    row = codes_r[to, h, tc : tc + 1, :]
+
+                @pl.when(h == 0)
+                def _():
+                    codes_w[to] = codes_r[to].astype(F32).reshape(HEADS, TILES, 128)
+
+                for tc in range(TILES):
+                    row = codes_w[to, h, tc : tc + 1, :]
                     hot[u * CAP : (u + 1) * CAP, tc * 128 : (tc + 1) * 128] = one_hot(row == rank_rows)
             rows = dot_nn(hot[:, :TOK], tab[h])
             stage_f[h, pl.ds(gi * GROUP, GROUP)] = rows.astype(BF16).reshape(GROUP, CAP, 4 * HD)
@@ -206,11 +225,13 @@
     lax.fori_loop(0, HEADS, gather_head, 0)
 
     for h in range(HEADS):
-        slot = jnp.zeros((TOK // 128, 128), F32)
+        dest_t[h] = jnp.transpose(jnp.broadcast_to(destrow[h], (128, SLOTS)))
+    for h in range(HEADS):
+        slot = jnp.zeros((TILES, 128), F32)
         for c in range(N):
-            code = codes_r[c, h]
+            code = codes_w[c, h]
             slot = slot + jnp.where(code > 0.0, code + (c * CAP - 1.0), 0.0)
-        for tc in range(TOK // 128):
+        for tc in range(TILES):
             slot_t[h, tc * 128 : (tc + 1) * 128, :] = jnp.transpose(
                 jnp.broadcast_to(slot[tc : tc + 1, :], (128, 128))
             )
@@ -220,6 +241,8 @@
     causal = lax.broadcasted_iota(jnp.int32, (BLK, BLK), 0) <= lax.broadcasted_iota(
         jnp.int32, (BLK, BLK), 1
     )
+
+    cent_in.wait()
 
     def cluster_head(h, carry):
         wait_all(h, fwd_copy, fwd_self)
@@ -297,69 +320,96 @@
 
     lax.fori_loop(0, HEADS, cluster_head, 0)
 
-    def tokens(h, tb):
-        wide = iota((BLK, 128), 1)
+    for h in range(HEADS):
+        fwd_copy(h, others, others, me).wait_send()
+    pltpu.make_async_copy(w_ref, w_ref, in_sem.at[3]).wait()
+
+    wide = iota((BLK, 128), 1)
+
+    def put_hot(h, tb, carry):
         rows_at = pl.ds(pl.multiple_of(tb * BLK, BLK), BLK)
         place = slot_t[h, rows_at, :]
         for pc in range(SLOTS // 128):
-            hot[:, pc * 128 : (pc + 1) * 128] = one_hot(place == wide + pc * 128.0)
-        rows = dot_nn(hot[...], recv_r[h].reshape(SLOTS, 3 * HD)).astype(BF16)
-        for a in range(3):
-            at = a * HEADS * HD + h * HD
-            z_ref[rows_at, at : at + HD] = rows[:, a * HD : (a + 1) * HD]
-
+            part_at, lane = divmod(pc * 128, 4 * HD)
+            block = one_hot(place == wide + pc * 128.0).reshape(BLK // CAP, CAP, 128)
+            some = pl.ds(part_at % 2 * (TOK // CAP) + tb * (BLK // CAP), BLK // CAP)
+            stage_f[part_at // 2, some, :, lane : lane + 128] = block
+        return carry
+
+    def tokens(h, tb):
+        acc = None
+        for part_at in range(SLOTS // (4 * HD)):
+            some = pl.ds(part_at % 2 * (TOK // CAP) + tb * (BLK // CAP), BLK // CAP)
+            hots = stage_f[part_at // 2, some].reshape(BLK, 4 * HD)
+            runs_at = 4 * HD // CAP
+            rows = recv_r[h, part_at * runs_at : (part_at + 1) * runs_at].reshape(4 * HD, 3 * HD)
+            term = dot_nn(hots, rows)
+            acc = term if acc is None else acc + term
+        return acc.astype(BF16)
+
+    lax.fori_loop(0, TOK // BLK, lambda tb, c: put_hot(0, tb, c), 0)
     wait_all(0, ret_copy, ret_self)
-    lax.fori_loop(0, TOK // BLK, lambda tb, c: (tokens(0, tb), c)[1], 0)
+
+    def first_part(tb, carry):
+        z = tokens(0, tb)
+        rows_at = pl.ds(pl.multiple_of(tb * BLK, BLK), BLK)
+
+        def one(d, inner):
+            w_d = w_ref[0, pl.ds(pl.multiple_of(d * 256, 256), 256), :]
+            first[d, rows_at, :] = dot_nt(z, w_d)
+            return inner
+
+        return lax.fori_loop(0, 2 * NY, one, carry)
+
+    lax.fori_loop(0, TOK // BLK, first_part, 0)
+    lax.fori_loop(0, TOK // BLK, lambda tb, c: put_hot(1, tb, c), 0)
     wait_all(1, ret_copy, ret_self)
 
+    def y_copy(src, dst, send_sem, recv_sem, other):
+        return pltpu.make_async_remote_copy(
+            src_ref=src, dst_ref=dst, send_sem=send_sem, recv_sem=recv_sem,
+            device_id=(me, other), device_id_type=MESH,
+        )
+
+    def onward(rc):
+        return (next_hd, y_next) if rc % 2 == 0 else (prev_hd, y_prev)
+
+    def back(rc):
+        return (prev_hd, y_prev) if rc % 2 == 0 else (next_hd, y_next)
+
     def core_copy(rc):
-        return pltpu.make_async_remote_copy(
-            src_ref=part.at[rc, 1 - core], dst_ref=part_r.at[rc],
-            send_sem=core_ss.at[rc], recv_sem=core_rs.at[rc],
-            device_id=(me, sibling), device_id_type=MESH,
-        )
+        return y_copy(part.at[rc, 1 - core], part_r.at[rc], core_ss.at[0], core_rs.at[rc], sibling)
 
     def hop_copy(rc):
-        return pltpu.make_async_remote_copy(
-            src_ref=p2.at[rc, y_far], dst_ref=hop_r.at[rc],
-            send_sem=hop_ss.at[rc], recv_sem=hop_rs.at[rc],
-            device_id=(me, next_hd if rc % 2 == 0 else prev_hd), device_id_type=MESH,
-        )
+        return y_copy(p2.at[rc, y_far], hop_r.at[rc], hop_ss.at[0], hop_rs.at[rc], onward(rc)[0])
 
     def dir_copy(rc):
-        return pltpu.make_async_remote_copy(
-            src_ref=p2.at[rc, y_prev if rc % 2 == 0 else y_next], dst_ref=dir_r.at[rc],
-            send_sem=dir_ss.at[rc], recv_sem=dir_rs.at[rc],
-            device_id=(me, prev_hd if rc % 2 == 0 else next_hd), device_id_type=MESH,
-        )
+        other, its_y = back(rc)
+        return y_copy(p2.at[rc, its_y], dir_r.at[rc], dir_ss.at[0], dir_rs.at[rc], other)
 
     def last_copy(rc):
-        return pltpu.make_async_remote_copy(
-            src_ref=hop_s.at[rc], dst_ref=last_r.at[rc],
-            send_sem=last_ss.at[rc], recv_sem=last_rs.at[rc],
-            device_id=(me, next_hd if rc % 2 == 0 else prev_hd), device_id_type=MESH,
-        )
+        return y_copy(hop_s.at[rc], last_r.at[rc], last_ss.at[0], last_rs.at[rc], onward(rc)[0])
+
+    per = BLK // RROWS
 
     def project(tb):
-        tokens(1, tb)
-        z = z_ref[tb * BLK : (tb + 1) * BLK, :]
-
-        def one(d, carry):
-            acc = None
-            for a in range(3):
-                term = dot_nt(
-                    z[:, a * HEADS * HD : (a + 1) * HEADS * HD],
-                    w_ref[a, pl.ds(pl.multiple_of(d * 256, 256), 256), :],
-                )
-                acc = term if acc is None else acc + term
-            low = acc.astype(BF16)
-            for piece in range(BLK // RROWS):
-                part[tb * (BLK // RROWS) + piece, lax.rem(d, 2), lax.div(d, 2)] = low[
-                    piece * RROWS : (piece + 1) * RROWS
-                ]
-            return carry
-
-        lax.fori_loop(0, 2 * NY, one, 0)
+        z = tokens(1, tb)
+
+        def half(side):
+            def one(yy, carry):
+                d = yy * 2 + side
+                w_d = w_ref[1, pl.ds(pl.multiple_of(d * 256, 256), 256), :]
+                low = (first[d, tb * BLK : (tb + 1) * BLK, :] + dot_nt(z, w_d)).astype(BF16)
+                for piece in range(per):
+                    part[tb * per + piece, side, yy] = low[piece * RROWS : (piece + 1) * RROWS]
+                return carry
+
+            lax.fori_loop(0, NY, one, 0)
+
+        half(1 - core)
+        for piece in range(per):
+            core_copy(tb * per + piece).start()
+        half(core)
 
     def merge(rc):
         core_copy(rc).wait_recv()
@@ -369,7 +419,7 @@
 
     def relay(rc):
         hop_copy(rc).wait_recv()
-        mine = p2[rc, y_next if rc % 2 == 0 else y_prev]
+        mine = p2[rc, onward(rc)[1]]
         hop_s[rc] = (hop_r[rc].astype(F32) + mine.astype(F32)).astype(BF16)
         last_copy(rc).start()
 
@@ -379,12 +429,9 @@
         total = p2[rc, my_y].astype(F32) + dir_r[rc].astype(F32) + last_r[rc].astype(F32)
         out_ref[rc * RROWS : (rc + 1) * RROWS, :] = total.astype(BF16)
 
-    per = BLK // RROWS
     for step in range(TOK // BLK + 3):
         if step < TOK // BLK:
             project(step)
-            for rc in range(step * per, (step + 1) * per):
-                core_copy(rc).start()
         if 1 <= step <= TOK // BLK:
             for rc in range((step - 1) * per, step * per):
                 merge(rc)
@@ -394,22 +441,13 @@
     for rc in range(RC):
         finish(rc)
 
-    def drain(n, carry):
-        @pl.when(n != SELF_STEP)
-        def _():
-            to = peer(n)
-            code_copy(n, to, me, to).wait_send()
-            for h in range(HEADS):
-                fwd_copy(h, n, me, to).wait_send()
-                ret_copy(h, n, me, to).wait_send()
-        return carry
-
-    lax.fori_loop(0, N, drain, 0)
-    for rc in range(RC):
-        core_copy(rc).wait_send()
-        hop_copy(rc).wait_send()
-        dir_copy(rc).wait_send()
-        last_copy(rc).wait_send()
+    code_copy(codes_s.at[others], codes_r.at[others], 0, me).wait_send()
+    for h in range(HEADS):
+        ret_copy(h, others, others, me).wait_send()
+    chunks = pl.ds(0, RC)
+    y_copy(part.at[chunks, 0], part_r, core_ss.at[0], core_rs.at[0], sibling).wait_send()
+    for sem in (hop_ss, dir_ss, last_ss):
+        y_copy(p2.at[chunks, 0], p2.at[chunks, 0], sem.at[0], hop_rs.at[0], next_hd).wait_send()
 
 
 def shards(queries, keys, values, out_grad, members, centroids, proj_weight):
@@ -421,12 +459,17 @@
             jax.ShapeDtypeStruct((TOK, HEADS * HD), BF16),
             jax.ShapeDtypeStruct((HEADS, 1, HD), F32),
         ),
-        in_specs=[vmem] * 7,
+        in_specs=[pl.BlockSpec(memory_space=pl.ANY)] * 7,
         out_specs=(vmem, vmem),
         scratch_shapes=[
+            pltpu.VMEM((HEADS, 1, W), jnp.int32),
+            pltpu.VMEM((HEADS, 1, HD), F32),
+            pltpu.VMEM((HEADS, 2048, 3 * HD), BF16),
+            dma((4,)),
+            pltpu.VMEM((N, HEADS, TILES, 128), F32),
             pltpu.VMEM((HEADS, TOK, 4 * HD), BF16),
-            pltpu.VMEM((N, HEADS, TOK // 128, 128), F32),
-            pltpu.VMEM((N, HEADS, TOK // 128, 128), F32),
+            pltpu.VMEM((N, HEADS * TILES, 128), BF16),
+            pltpu.VMEM((N, HEADS * TILES, 128), BF16),
             pltpu.VMEM((HEADS, 1, SLOTS), F32),
             pltpu.VMEM((HEADS, SLOTS, 128), F32),
             pltpu.VMEM((HEADS, TOK, 128), F32),
@@ -442,7 +485,7 @@
             pltpu.VMEM((HD, W), BF16),
             pltpu.VMEM((HEADS, N, CAP, 3 * HD), BF16),
             pltpu.VMEM((HEADS, N, CAP, 3 * HD), BF16),
-            pltpu.VMEM((TOK, 3 * HEADS * HD), BF16),
+            pltpu.VMEM((2 * NY, TOK, 256), F32),
             pltpu.VMEM((RC, 2, NY, RROWS, 256), BF16),
             pltpu.VMEM((RC, NY, RROWS, 256), BF16),
             pltpu.VMEM((RC, NY, RROWS, 256), BF16),
@@ -450,14 +493,14 @@
             pltpu.VMEM((RC, RROWS, 256), BF16),
             pltpu.VMEM((RC, RROWS, 256), BF16),
             pltpu.VMEM((RC, RROWS, 256), BF16),
-            dma((N,)), dma((N,)),
-            dma((HEADS, N)), dma((HEADS, N)),
-            dma((HEADS, N)), dma((HEADS, N)),
+            dma((1,)), dma((NZ,)),
+            dma((HEADS,)), dma((HEADS,)),
+            dma((HEADS,)), dma((HEADS,)),
             dma((2, HEADS)),
-            dma((RC,)), dma((RC,)),
-            dma((RC,)), dma((RC,)),
-            dma((RC,)), dma((RC,)),
-            dma((RC,)), dma((RC,)),
+            dma((1,)), dma((RC,)),
+            dma((1,)), dma((RC,)),
+            dma((1,)), dma((RC,)),
+            dma((1,)), dma((RC,)),
         ],
         compiler_params=pltpu.CompilerParams(
             collective_id=0, has_side_effects=True, vmem_limit_bytes=60 * 1024 * 1024

time: 219 us -> 206 us (0.941); the launches traced: 219 us -> 202 us
  Pallas kernels: 215 us -> 199 us
    pallas_call x1, Pallas kernels: 215 us -> 199 us  [shards(): pl.pallas_call(kernel, out_shape=(jax.ShapeDtypeStruct((TOK, HEADS * HD),...]
where the time goes in v2:
time: 206 us; the launch traced here: 202 us
  Pallas kernels  199 us (97%)
  local copies, waits for them, and re-layouts  3.07 us (1%)
    pallas_call x1, Pallas kernels, shards(): pl.pallas_call(kernel, out_shape=(jax.ShapeDtypeStruct((TOK, HEADS * HD),...  199 us

profile of v2, /device:TPU:8, one launch (start us, length us, event | category | flops | bytes accessed | tf_op | source)
XLA Modules:
  0.0 202.2 jit_solution(3762416094407953033)
XLA Ops:
  0.6 198.5 %shard_map.86 = (bf16[1024,256]{1,0:T(8,128)(2,1)}, f32[2,1,128]{2,1,0:T(1,128)}) custom-call(bf16[1024,256]{1,0:T(8,128)(2,1)} %q_hbm.1, bf16[1024,256]{1,0:T(8,128)(2,1)} %k_hbm.1, bf16[1024,256]{1,0:T(8,128)(2,1)} %v_hbm.1, bf16[1024,256]{1,0:T(8,128)(2,1)} %g_hbm.1, s32[2,1,1024]{2,1,0:T(1,128)} %mem_hbm.1, f32[2,1,128]{2,1,0:T(1,128)} %cent_hbm.1, ...), custom_call_target="tpu_custom_call" | custom-call | tf_op jit(solution)/shard_map/pallas_call | solution.py:456
  199.1 1.9 copy.11
  201.0 1.2 copy.12

commit v3 on v2

--- a/solution.py
+++ b/solution.py
@@ -24,10 +24,10 @@
 SLOTS = N * CAP
 GROUP = 4
 BLK = 256
-RC = 8
-RROWS = TOK // RC
+HALF = TOK // 2
 TILES = TOK // 128
-SELF_STEP = (NZ - 1) * NX
+LEVELS = NZ // 2
+SELF_STEP = 1
 
 
 def one_hot(mask):
@@ -51,7 +51,7 @@
     out_ref, newc_ref,
     mem_ref, cent_ref, w_ref, in_sem, codes_w, tab, codes_s, codes_r, destrow, dest_t, slot_t, hot,
     stage_f, recv_f, x_ref, y_ref, dk_ref, dv_ref, p_scr, d_scr, k_t,
-    stage_r, recv_r, first, part, part_r, p2, hop_r, hop_s, dir_r, last_r,
+    stage_r, recv_r, first, z_sum, z_ref, own, part, part_r, p2, hop_r, hop_s, dir_r, last_r,
     code_ss, code_rs, fwd_ss, fwd_rs, ret_ss, ret_rs, self_sem,
     core_ss, core_rs, hop_ss, hop_rs, dir_ss, dir_rs, last_ss, last_rs,
 ):
@@ -66,13 +66,14 @@
     next_hd = y_next * 2 + core
     prev_hd = y_prev * 2 + core
 
+    def level_z(level, side):
+        dz = jnp.where(side == 0, NZ // 2 - level, jnp.where(level == 0, 0, NZ // 2 + level))
+        return lax.rem(my_z + dz, NZ)
+
     def peer(n):
-        step = lax.div(n, NX)
-        dx = lax.rem(n, NX)
-        half = lax.div(step, 2)
-        odd = lax.rem(step, 2)
-        dz = jnp.where(step == NZ - 1, 0, jnp.where(odd == 1, NZ - 1 - half, 1 + half))
-        return lax.rem(my_z + dz, NZ) * NX + lax.rem(my_x + dx, NX)
+        in_level = lax.rem(n, 2 * NX)
+        dx = lax.div(in_level, 2)
+        return level_z(lax.div(n, 2 * NX), lax.rem(in_level, 2)) * NX + lax.rem(my_x + dx, NX)
 
     barrier = pltpu.get_barrier_semaphore()
 
@@ -131,10 +132,7 @@
         @pl.when(n != SELF_STEP)
         def _():
             to = peer(n)
-            step = lax.div(n, NX)
-            swap = step + 1 - 2 * lax.rem(step, 2)
-            there = jnp.where(step < NZ - 2, swap, step)
-            code_copy(codes_s.at[to], codes_r.at[me], there, to).start()
+            code_copy(codes_s.at[to], codes_r.at[me], lax.div(n, 2 * NX), to).start()
         return carry
 
     def wait_codes(step, count):
@@ -160,10 +158,10 @@
             device_id=(other, hd), device_id_type=MESH,
         )
 
-    def ret_copy(h, src, dst, other):
+    def ret_copy(h, src, dst, other, step):
         return pltpu.make_async_remote_copy(
             src_ref=stage_r.at[h, src], dst_ref=recv_r.at[h, dst],
-            send_sem=ret_ss.at[h], recv_sem=ret_rs.at[h],
+            send_sem=ret_ss.at[h], recv_sem=ret_rs.at[h, step],
             device_id=(other, hd), device_id_type=MESH,
         )
 
@@ -173,37 +171,39 @@
     def ret_self(h):
         return pltpu.make_async_copy(stage_r.at[h, SELF_STEP], recv_r.at[h, me], self_sem.at[1, h])
 
-    def launch(h, gi, copy_of, self_of):
+    def launch(gi, copy_of, self_copy):
         for u in range(GROUP):
             n = gi * GROUP + u
             to = peer(n)
 
             @pl.when(n != SELF_STEP)
             def _():
-                copy_of(h, n, me, to).start()
+                copy_of(n, to).start()
 
             @pl.when(n == SELF_STEP)
             def _():
-                self_of(h).start()
+                self_copy.start()
 
     others = pl.ds(0, N - 1)
 
-    def wait_all(h, copy_of, self_of):
-        copy_of(h, others, others, me).wait_recv()
-        self_of(h).wait()
+    def wait_ret(h, step):
+        some = pl.ds(0, 2 * NX - (step == 0))
+        ret_copy(h, some, some, me, step).wait_recv()
+        if step == 0:
+            ret_self(h).wait()
 
     rank_rows = iota((CAP, 128), 0) + 1.0
     lanes = iota((CAP, 128), 1)
 
     def gather_head(h, carry):
         def group(gi, inner):
-            @pl.when((h == 0) & (gi < NZ - 1))
+            @pl.when((h == 0) & (gi == 0))
             def _():
-                wait_codes(gi, NX)
-
-            @pl.when((h == 0) & (gi == NZ - 1))
+                wait_codes(0, 2 * NX - 1)
+
+            @pl.when((h == 0) & (gi > 0) & (lax.rem(gi, 2) == 0))
             def _():
-                wait_codes(gi, NX - 1)
+                wait_codes(lax.div(gi, 2), 2 * NX)
 
             for u in range(GROUP):
                 to = peer(gi * GROUP + u)
@@ -217,7 +217,7 @@
                     hot[u * CAP : (u + 1) * CAP, tc * 128 : (tc + 1) * 128] = one_hot(row == rank_rows)
             rows = dot_nn(hot[:, :TOK], tab[h])
             stage_f[h, pl.ds(gi * GROUP, GROUP)] = rows.astype(BF16).reshape(GROUP, CAP, 4 * HD)
-            launch(h, gi, fwd_copy, fwd_self)
+            launch(gi, lambda n, to: fwd_copy(h, n, me, to), fwd_self(h))
             return inner
 
         return lax.fori_loop(0, N // GROUP, group, carry)
@@ -245,7 +245,8 @@
     cent_in.wait()
 
     def cluster_head(h, carry):
-        wait_all(h, fwd_copy, fwd_self)
+        fwd_copy(h, others, others, me).wait_recv()
+        fwd_self(h).wait()
 
         def order(ib, sums):
             place = iota((BLK, 128), 0) + (ib * BLK).astype(F32)
@@ -313,7 +314,7 @@
                     )
             rows = dot_nn(hot[:, :W], y_ref[...])
             stage_r[h, pl.ds(gi * GROUP, GROUP)] = rows.astype(BF16).reshape(GROUP, CAP, 3 * HD)
-            launch(h, gi, ret_copy, ret_self)
+            launch(gi, lambda n, to: ret_copy(h, n, me, to, lax.div(gi, 2)), ret_self(h))
             return inner
 
         return lax.fori_loop(0, N // GROUP, group, carry)
@@ -347,8 +348,28 @@
             acc = term if acc is None else acc + term
         return acc.astype(BF16)
 
+    def tokens_step(step):
+        for half in range(2):
+            term = None
+            for side in range(2):
+                at_z = level_z(step, side)
+                lane = pl.ds(pl.multiple_of(lax.rem(at_z, 2) * (NX * CAP), NX * CAP), NX * CAP)
+                rows = recv_r[1, pl.ds(at_z * NX, NX)].reshape(NX * CAP, 3 * HD)
+                low = lax.rem(lax.div(at_z, 2), 2) * (TOK // CAP) + half * (HALF // CAP)
+                hots = stage_f[lax.div(at_z, 4), pl.ds(low, HALF // CAP), :, lane].reshape(HALF, NX * CAP)
+                more = dot_nn(hots, rows)
+                term = more if term is None else term + more
+            at = slice(half * HALF, (half + 1) * HALF)
+            if step == 0:
+                z_sum[at, :] = term
+            elif step < LEVELS - 1:
+                z_sum[at, :] += term
+            else:
+                z_ref[at, :] = (z_sum[at, :] + term).astype(BF16)
+
     lax.fori_loop(0, TOK // BLK, lambda tb, c: put_hot(0, tb, c), 0)
-    wait_all(0, ret_copy, ret_self)
+    for step in range(LEVELS):
+        wait_ret(0, step)
 
     def first_part(tb, carry):
         z = tokens(0, tb)
@@ -363,7 +384,9 @@
 
     lax.fori_loop(0, TOK // BLK, first_part, 0)
     lax.fori_loop(0, TOK // BLK, lambda tb, c: put_hot(1, tb, c), 0)
-    wait_all(1, ret_copy, ret_self)
+    for step in range(LEVELS):
+        wait_ret(1, step)
+        tokens_step(step)
 
     def y_copy(src, dst, send_sem, recv_sem, other):
         return pltpu.make_async_remote_copy(
@@ -371,89 +394,97 @@
             device_id=(me, other), device_id_type=MESH,
         )
 
-    def onward(rc):
-        return (next_hd, y_next) if rc % 2 == 0 else (prev_hd, y_prev)
-
-    def back(rc):
-        return (prev_hd, y_prev) if rc % 2 == 0 else (next_hd, y_next)
-
-    def core_copy(rc):
-        return y_copy(part.at[rc, 1 - core], part_r.at[rc], core_ss.at[0], core_rs.at[rc], sibling)
-
-    def hop_copy(rc):
-        return y_copy(p2.at[rc, y_far], hop_r.at[rc], hop_ss.at[0], hop_rs.at[rc], onward(rc)[0])
-
-    def dir_copy(rc):
-        other, its_y = back(rc)
-        return y_copy(p2.at[rc, its_y], dir_r.at[rc], dir_ss.at[0], dir_rs.at[rc], other)
-
-    def last_copy(rc):
-        return y_copy(hop_s.at[rc], last_r.at[rc], last_ss.at[0], last_rs.at[rc], onward(rc)[0])
-
-    per = BLK // RROWS
-
-    def project(tb):
-        z = tokens(1, tb)
-
-        def half(side):
-            def one(yy, carry):
-                d = yy * 2 + side
-                w_d = w_ref[1, pl.ds(pl.multiple_of(d * 256, 256), 256), :]
-                low = (first[d, tb * BLK : (tb + 1) * BLK, :] + dot_nt(z, w_d)).astype(BF16)
-                for piece in range(per):
-                    part[tb * per + piece, side, yy] = low[piece * RROWS : (piece + 1) * RROWS]
-                return carry
-
-            lax.fori_loop(0, NY, one, 0)
-
-        half(1 - core)
-        for piece in range(per):
-            core_copy(tb * per + piece).start()
-        half(core)
-
-    def merge(rc):
-        core_copy(rc).wait_recv()
-        p2[rc] = (part[rc, core].astype(F32) + part_r[rc].astype(F32)).astype(BF16)
-        hop_copy(rc).start()
-        dir_copy(rc).start()
-
-    def relay(rc):
-        hop_copy(rc).wait_recv()
-        mine = p2[rc, onward(rc)[1]]
-        hop_s[rc] = (hop_r[rc].astype(F32) + mine.astype(F32)).astype(BF16)
-        last_copy(rc).start()
-
-    def finish(rc):
-        dir_copy(rc).wait_recv()
-        last_copy(rc).wait_recv()
-        total = p2[rc, my_y].astype(F32) + dir_r[rc].astype(F32) + last_r[rc].astype(F32)
-        out_ref[rc * RROWS : (rc + 1) * RROWS, :] = total.astype(BF16)
-
-    for step in range(TOK // BLK + 3):
-        if step < TOK // BLK:
-            project(step)
-        if 1 <= step <= TOK // BLK:
-            for rc in range((step - 1) * per, step * per):
-                merge(rc)
-        if 2 <= step <= TOK // BLK + 1:
-            for rc in range((step - 2) * per, (step - 1) * per):
-                relay(rc)
-    for rc in range(RC):
-        finish(rc)
+    blocks = (y_far, y_next, y_prev, my_y)
+    halves = (slice(0, HALF), slice(HALF, TOK))
+
+    def core_copy(r, f):
+        return y_copy(
+            part.at[r, halves[f]], part_r.at[r, halves[f]], core_ss.at[0], core_rs.at[r, f], sibling
+        )
+
+    def hop_copy(f):
+        return y_copy(
+            p2.at[0, halves[f]], hop_r.at[f], hop_ss.at[0], hop_rs.at[f], (next_hd, prev_hd)[f]
+        )
+
+    def dir_copy(f):
+        return y_copy(
+            p2.at[2 - f, halves[f]], dir_r.at[f], dir_ss.at[0], dir_rs.at[f], (prev_hd, next_hd)[f]
+        )
+
+    def last_copy(f):
+        return y_copy(hop_s.at[f], last_r.at[f], last_ss.at[0], last_rs.at[f], (next_hd, prev_hd)[f])
+
+    def block(r, side, half):
+        d = blocks[r] * 2 + side
+        w_d = w_ref[1, pl.ds(pl.multiple_of(d * 256, 256), 256), :]
+        return first[d, half, :] + dot_nt(z_ref[half, :], w_d)
+
+    def theirs(r):
+        for f in range(2):
+            part[r, halves[f], :] = block(r, 1 - core, halves[f]).astype(BF16)
+            core_copy(r, f).start()
+
+    def ours(r):
+        for half in halves:
+            own[half, :] = block(r, core, half)
+
+    def merge(r, f):
+        core_copy(r, f).wait_recv()
+        half = halves[f]
+        p2[r, half, :] = (own[half, :] + part_r[r, half, :].astype(F32)).astype(BF16)
+
+    def relay(f):
+        hop_copy(f).wait_recv()
+        hop_s[f] = (hop_r[f].astype(F32) + p2[1 + f, halves[f], :].astype(F32)).astype(BF16)
+        last_copy(f).start()
+
+    theirs(0)
+    ours(0)
+    theirs(1)
+    for f in range(2):
+        merge(0, f)
+        hop_copy(f).start()
+    theirs(2)
+    ours(1)
+    merge(1, 1)
+    dir_copy(1).start()
+    merge(1, 0)
+    ours(2)
+    merge(2, 0)
+    dir_copy(0).start()
+    merge(2, 1)
+    theirs(3)
+    relay(0)
+    relay(1)
+    ours(3)
+    for f in range(2):
+        core_copy(3, f).wait_recv()
+        own[halves[f], :] += part_r[3, halves[f], :].astype(F32)
+    for f in range(2):
+        dir_copy(f).wait_recv()
+        own[halves[f], :] += dir_r[f].astype(F32)
+    for f in range(2):
+        last_copy(f).wait_recv()
+        out_ref[halves[f], :] = (own[halves[f], :] + last_r[f].astype(F32)).astype(BF16)
 
     code_copy(codes_s.at[others], codes_r.at[others], 0, me).wait_send()
     for h in range(HEADS):
-        ret_copy(h, others, others, me).wait_send()
-    chunks = pl.ds(0, RC)
-    y_copy(part.at[chunks, 0], part_r, core_ss.at[0], core_rs.at[0], sibling).wait_send()
+        ret_copy(h, others, others, me, 0).wait_send()
+    y_copy(part, part_r, core_ss.at[0], core_rs.at[0, 0], sibling).wait_send()
     for sem in (hop_ss, dir_ss, last_ss):
-        y_copy(p2.at[chunks, 0], p2.at[chunks, 0], sem.at[0], hop_rs.at[0], next_hd).wait_send()
+        y_copy(hop_s, hop_r, sem.at[0], hop_rs.at[0], next_hd).wait_send()
+
+
+def hand_over(grad_ref, cent_ref, out_ref, newc_ref):
+    out_ref[...] = grad_ref[...]
+    newc_ref[...] = cent_ref[...]
 
 
 def shards(queries, keys, values, out_grad, members, centroids, proj_weight):
     vmem = pl.BlockSpec(memory_space=pltpu.VMEM)
     dma = pltpu.SemaphoreType.DMA
-    return pl.pallas_call(
+    results = pl.pallas_call(
         kernel,
         out_shape=(
             jax.ShapeDtypeStruct((TOK, HEADS * HD), BF16),
@@ -486,26 +517,38 @@
             pltpu.VMEM((HEADS, N, CAP, 3 * HD), BF16),
             pltpu.VMEM((HEADS, N, CAP, 3 * HD), BF16),
             pltpu.VMEM((2 * NY, TOK, 256), F32),
-            pltpu.VMEM((RC, 2, NY, RROWS, 256), BF16),
-            pltpu.VMEM((RC, NY, RROWS, 256), BF16),
-            pltpu.VMEM((RC, NY, RROWS, 256), BF16),
-            pltpu.VMEM((RC, RROWS, 256), BF16),
-            pltpu.VMEM((RC, RROWS, 256), BF16),
-            pltpu.VMEM((RC, RROWS, 256), BF16),
-            pltpu.VMEM((RC, RROWS, 256), BF16),
-            dma((1,)), dma((NZ,)),
+            pltpu.VMEM((TOK, 3 * HD), F32),
+            pltpu.VMEM((TOK, 3 * HD), BF16),
+            pltpu.VMEM((TOK, 256), F32),
+            pltpu.VMEM((NY, TOK, 256), BF16),
+            pltpu.VMEM((NY, TOK, 256), BF16),
+            pltpu.VMEM((3, TOK, 256), BF16),
+            pltpu.VMEM((2, HALF, 256), BF16),
+            pltpu.VMEM((2, HALF, 256), BF16),
+            pltpu.VMEM((2, HALF, 256), BF16),
+            pltpu.VMEM((2, HALF, 256), BF16),
+            dma((1,)), dma((LEVELS,)),
             dma((HEADS,)), dma((HEADS,)),
-            dma((HEADS,)), dma((HEADS,)),
+            dma((HEADS,)), dma((HEADS, LEVELS)),
             dma((2, HEADS)),
-            dma((1,)), dma((RC,)),
-            dma((1,)), dma((RC,)),
-            dma((1,)), dma((RC,)),
-            dma((1,)), dma((RC,)),
+            dma((1,)), dma((NY, 2)),
+            dma((1,)), dma((2,)),
+            dma((1,)), dma((2,)),
+            dma((1,)), dma((2,)),
         ],
         compiler_params=pltpu.CompilerParams(
             collective_id=0, has_side_effects=True, vmem_limit_bytes=60 * 1024 * 1024
         ),
     )(queries, keys, values, out_grad, members, centroids, proj_weight)
+    return pl.pallas_call(
+        hand_over,
+        out_shape=(
+            jax.ShapeDtypeStruct((TOK, HEADS * HD), BF16),
+            jax.ShapeDtypeStruct((HEADS, 1, HD), F32),
+        ),
+        in_specs=[vmem] * 2,
+        out_specs=(vmem, vmem),
+    )(*results)
 
 
 def solution(mesh):

time: 206 us -> 204 us (level)
  local copies, waits for them, and re-layouts: 3.07 us -> 0 us
  Pallas kernels: 199 us -> 202 us
    unnamed x2 -> x0, local copies, waits for them, and re-layouts: 3.07 us -> none
where the time goes in v3:
time: 204 us; the launch traced here: 202 us
  Pallas kernels  202 us (99%)
    pallas_call x1, Pallas kernels, shards(): pl.pallas_call(kernel, out_shape=(jax.ShapeDtypeStruct((TOK, HEADS * HD),...  200 us

profile of v3, /device:TPU:8, one launch (start us, length us, event | category | flops | bytes accessed | tf_op | source)
XLA Modules:
  0.0 202.2 jit_solution(10422374402329961844)
XLA Ops:
  0.6 199.7 %shard_map.86 = (bf16[1024,256]{1,0:T(8,128)(2,1)}, f32[2,1,128]{2,1,0:T(1,128)}) custom-call(bf16[1024,256]{1,0:T(8,128)(2,1)} %q_hbm.1, bf16[1024,256]{1,0:T(8,128)(2,1)} %k_hbm.1, bf16[1024,256]{1,0:T(8,128)(2,1)} %v_hbm.1, bf16[1024,256]{1,0:T(8,128)(2,1)} %g_hbm.1, s32[2,1,1024]{2,1,0:T(1,128)} %mem_hbm.1, f32[2,1,128]{2,1,0:T(1,128)} %cent_hbm.1, ...), custom_call_target="tpu_custom_call" | custom-call | tf_op jit(solution)/shard_map/pallas_call | solution.py:487
  200.4 1.9 shard_map.87

commit v4 on v3

--- a/solution.py
+++ b/solution.py
@@ -161,7 +161,7 @@
     def ret_copy(h, src, dst, other, step):
         return pltpu.make_async_remote_copy(
             src_ref=stage_r.at[h, src], dst_ref=recv_r.at[h, dst],
-            send_sem=ret_ss.at[h], recv_sem=ret_rs.at[h, step],
+            send_sem=ret_ss.at[h, step], recv_sem=ret_rs.at[h, step],
             device_id=(other, hd), device_id_type=MESH,
         )
 
@@ -185,6 +185,10 @@
                 self_copy.start()
 
     others = pl.ds(0, N - 1)
+
+    def sent_ret(h, step):
+        some = pl.ds(0, 2 * NX - (step == 0))
+        ret_copy(h, some, some, me, step).wait_send()
 
     def wait_ret(h, step):
         some = pl.ds(0, 2 * NX - (step == 0))
@@ -314,6 +318,11 @@
                     )
             rows = dot_nn(hot[:, :W], y_ref[...])
             stage_r[h, pl.ds(gi * GROUP, GROUP)] = rows.astype(BF16).reshape(GROUP, CAP, 3 * HD)
+
+            @pl.when((h == HEADS - 1) & (gi == 2 * (LEVELS - 1)))
+            def _():
+                sent_ret(HEADS - 1, 0)
+
             launch(gi, lambda n, to: ret_copy(h, n, me, to, lax.div(gi, 2)), ret_self(h))
             return inner
 
@@ -470,7 +479,9 @@
 
     code_copy(codes_s.at[others], codes_r.at[others], 0, me).wait_send()
     for h in range(HEADS):
-        ret_copy(h, others, others, me, 0).wait_send()
+        for step in range(LEVELS):
+            if (h, step) != (HEADS - 1, 0):
+                sent_ret(h, step)
     y_copy(part, part_r, core_ss.at[0], core_rs.at[0, 0], sibling).wait_send()
     for sem in (hop_ss, dir_ss, last_ss):
         y_copy(hop_s, hop_r, sem.at[0], hop_rs.at[0], next_hd).wait_send()
@@ -529,7 +540,7 @@
             pltpu.VMEM((2, HALF, 256), BF16),
             dma((1,)), dma((LEVELS,)),
             dma((HEADS,)), dma((HEADS,)),
-            dma((HEADS,)), dma((HEADS, LEVELS)),
+            dma((HEADS, LEVELS)), dma((HEADS, LEVELS)),
             dma((2, HEADS)),
             dma((1,)), dma((NY, 2)),
             dma((1,)), dma((2,)),

time: 204 us -> 204 us (level)
  no operation moved by 1% of the time
where the time goes in v4:
time: 204 us; the launch traced here: 202 us
  Pallas kernels  202 us (99%)
    pallas_call x1, Pallas kernels, shards(): pl.pallas_call(kernel, out_shape=(jax.ShapeDtypeStruct((TOK, HEADS * HD),...  200 us

profile of v4, /device:TPU:8, one launch (start us, length us, event | category | flops | bytes accessed | tf_op | source)
XLA Modules:
  0.0 202.3 jit_solution(8952271311091593174)
XLA Ops:
  0.6 199.8 %shard_map.86 = (bf16[1024,256]{1,0:T(8,128)(2,1)}, f32[2,1,128]{2,1,0:T(1,128)}) custom-call(bf16[1024,256]{1,0:T(8,128)(2,1)} %q_hbm.1, bf16[1024,256]{1,0:T(8,128)(2,1)} %k_hbm.1, bf16[1024,256]{1,0:T(8,128)(2,1)} %v_hbm.1, bf16[1024,256]{1,0:T(8,128)(2,1)} %g_hbm.1, s32[2,1,1024]{2,1,0:T(1,128)} %mem_hbm.1, f32[2,1,128]{2,1,0:T(1,128)} %cent_hbm.1, ...), custom_call_target="tpu_custom_call" | custom-call | tf_op jit(solution)/shard_map/pallas_call | solution.py:498
  200.4 1.9 shard_map.87

commit v5 on v3

--- a/solution.py
+++ b/solution.py
@@ -77,18 +77,19 @@
 
     barrier = pltpu.get_barrier_semaphore()
 
-    def greet(n, carry):
-        @pl.when(n != SELF_STEP)
-        def _():
-            pl.semaphore_signal(barrier, inc=1, device_id=(peer(n), hd), device_id_type=MESH)
-        return carry
-
-    lax.fori_loop(0, N, greet, 0)
+    mem_in = pltpu.make_async_copy(mem_hbm, mem_ref, in_sem.at[0])
+    mem_in.start()
+    rings = [(lax.rem(my_z + dz, NZ) * NX, LEVELS - min(dz, NZ - dz) if dz else 0) for dz in range(NZ)]
+    across = [lax.rem(my_x + dx, NX) for dx in range(NX)]
+    far_first = (4, 3, 5, 2, 6, 1, 7, 0)
+    peers = [
+        (rings[dz][0] + across[dx], rings[dz][1]) for dz in far_first for dx in range(NX) if dz or dx
+    ]
+    for to, _ in peers:
+        pl.semaphore_signal(barrier, inc=1, device_id=(to, hd), device_id_type=MESH)
     for other in (sibling, next_hd, prev_hd):
         pl.semaphore_signal(barrier, inc=1, device_id=(me, other), device_id_type=MESH)
 
-    mem_in = pltpu.make_async_copy(mem_hbm, mem_ref, in_sem.at[0])
-    mem_in.start()
     cent_in = pltpu.make_async_copy(cent_hbm, cent_ref, in_sem.at[1])
     cent_in.start()
     for h in range(HEADS):
@@ -128,27 +129,15 @@
             device_id=(other, hd), device_id_type=MESH,
         )
 
-    def send_codes(n, carry):
-        @pl.when(n != SELF_STEP)
-        def _():
-            to = peer(n)
-            code_copy(codes_s.at[to], codes_r.at[me], lax.div(n, 2 * NX), to).start()
-        return carry
+    for to, level in peers:
+        code_copy(codes_s.at[to], codes_r.at[me], level, to).start()
 
     def wait_codes(step, count):
         some = pl.ds(0, count)
         code_copy(codes_s.at[some], codes_r.at[some], step, me).wait_recv()
 
-    lax.fori_loop(0, N, send_codes, 0)
     codes_r[me] = codes_s[me]
 
-    for h in range(HEADS):
-        start, count = runs[h]
-        slot = lax.broadcasted_iota(jnp.int32, (N, SLOTS), 1)
-        dev2 = lax.broadcasted_iota(jnp.int32, (N, SLOTS), 0)
-        rank_at = (slot & (CAP - 1)).astype(F32)
-        place = jnp.where(rank_at < count, start + rank_at, -1.0)
-        destrow[h] = jnp.sum(jnp.where((slot >> 6) == dev2, place, 0.0), axis=0, keepdims=True)
     pltpu.make_async_copy(tab, tab, in_sem.at[2]).wait()
 
     def fwd_copy(h, src, dst, other):
@@ -224,6 +213,13 @@
 
     lax.fori_loop(0, HEADS, gather_head, 0)
 
+    for h in range(HEADS):
+        start, count = runs[h]
+        slot = lax.broadcasted_iota(jnp.int32, (N, SLOTS), 1)
+        dev2 = lax.broadcasted_iota(jnp.int32, (N, SLOTS), 0)
+        rank_at = (slot & (CAP - 1)).astype(F32)
+        place = jnp.where(rank_at < count, start + rank_at, -1.0)
+        destrow[h] = jnp.sum(jnp.where((slot >> 6) == dev2, place, 0.0), axis=0, keepdims=True)
     for h in range(HEADS):
         dest_t[h] = jnp.transpose(jnp.broadcast_to(destrow[h], (128, SLOTS)))
     for h in range(HEADS):

time: 204 us -> 204 us (level)
  no operation moved by 1% of the time
where the time goes in v5:
time: 204 us; the launch traced here: 202 us
  Pallas kernels  201 us (99%)
    pallas_call x1, Pallas kernels, shards(): pl.pallas_call(kernel, out_shape=(jax.ShapeDtypeStruct((TOK, HEADS * HD),...  200 us

profile of v5, /device:TPU:8, one launch (start us, length us, event | category | flops | bytes accessed | tf_op | source)
XLA Modules:
  0.0 202.1 jit_solution(8380397096512147089)
XLA Ops:
  0.6 199.6 %shard_map.86 = (bf16[1024,256]{1,0:T(8,128)(2,1)}, f32[2,1,128]{2,1,0:T(1,128)}) custom-call(bf16[1024,256]{1,0:T(8,128)(2,1)} %q_hbm.1, bf16[1024,256]{1,0:T(8,128)(2,1)} %k_hbm.1, bf16[1024,256]{1,0:T(8,128)(2,1)} %v_hbm.1, bf16[1024,256]{1,0:T(8,128)(2,1)} %g_hbm.1, s32[2,1,1024]{2,1,0:T(1,128)} %mem_hbm.1, f32[2,1,128]{2,1,0:T(1,128)} %cent_hbm.1, ...), custom_call_target="tpu_custom_call" | custom-call | tf_op jit(solution)/shard_map/pallas_call | solution.py:483
  200.2 1.9 shard_map.87
